TPU v7x, 32 devices: a whole 2x2x4 slice. The times are simulated.
32 devices in a mesh: gx: 8 (over y, x, core), gy: 4 (over z).
Axes of the slice: x: 2, y: 2, z: 4, core: 2. Of those that a mesh axis runs over, the one named last changes fastest.
Arguments:
- fields: float32 [6, 128, 128, 128], P(None, 'gx', 'gy'), may hold values from -0.0029296875 to 0.0029296875
- region: int32 [128, 128, 128], P('gx', 'gy'), may hold values from 0 to 15
- eps_table: float32 [16], replicated, may hold values from 1 to 2
Outputs:
- advanced: float32 [6, 128, 128, 128], P(None, 'gx', 'gy')
All inputs are finite; a program needn't handle non-finite values.
Results may differ from a plain program's by a relative error of at most 0.0003.
Values sent between devices are 32-bit elements; how exact they have to be, the bound alone decides.
A program may use at most 128 MiB of HBM per device.

v0:
```python
import jax
import jax.numpy as jnp
from jax import lax
from jax.sharding import PartitionSpec as P

plane_ratio = 32.0
depth_ratio = 0.5


def padded(cells, sides, width):
    for axis, dim in sides:
        count = lax.axis_size(axis)
        ends = count - 1
        head = lax.slice_in_dim(cells, 0, width, axis=dim)
        tail = lax.slice_in_dim(cells, cells.shape[dim] - width, cells.shape[dim], axis=dim)
        cells = jnp.concatenate(
            [
                lax.ppermute(tail, axis, [(i, (i + 1) % count) for i in range(ends)]),
                cells,
                lax.ppermute(head, axis, [((i + 1) % count, i) for i in range(ends)]),
            ],
            axis=dim,
        )
    return cells


def from_behind(block, axis, distance):
    devices = range(lax.axis_size(axis))
    route = [(i - distance, i) for i in devices if i - distance in devices]
    return lax.ppermute(block, axis, route)


def roll_next(values, along_axis):
    return jnp.roll(values, -1, along_axis) - values


def roll_prev(values, along_axis):
    return values - jnp.roll(values, 1, along_axis)


def depth_next(values):
    tail_zeros = jnp.zeros_like(values[..., :1])
    return jnp.concatenate([values[..., 1:], tail_zeros], axis=-1) - values


def depth_prev(values):
    head_zeros = jnp.zeros_like(values[..., :1])
    return values - jnp.concatenate([head_zeros, values[..., :-1]], axis=-1)


def crop_rim(values):
    return values[1:-1, 1:-1]


def extend(stacked):
    return padded(stacked, (("gx", 1), ("gy", 2)), 1)


def lookup_scale(region, eps_table):
    inverse = 1.0 / eps_table
    labels = jnp.arange(eps_table.shape[0], dtype=jnp.int32)
    matches = region[None] == labels[:, None, None, None]
    return jnp.sum(jnp.where(matches, inverse[:, None, None, None], jnp.float32(0.0)), axis=0)


def take_row(values, position, dim):
    if dim == 0:
        return values[position]
    return values[:, position]


def local_sweeps(coupling, right_side, dim, is_first, is_last):
    length = coupling.shape[dim]
    zeros_row = jnp.zeros_like(take_row(coupling, 0, dim))
    upper_list = []
    terms_list = []
    carried_upper = zeros_row
    carried_terms = (zeros_row, zeros_row, zeros_row)
    for position in range(length):
        local_k = take_row(coupling, position, dim)
        if position == 0:
            lower_row = zeros_row
            diag_row = 1.0 + local_k * jnp.where(is_first, 1.0, 2.0)
            left_term = jnp.where(is_first, zeros_row, -local_k)
        else:
            lower_row = -local_k
            diag_row = 1.0 + local_k * 2.0
            left_term = zeros_row
        if position == length - 1:
            upper_row = zeros_row
            right_term = jnp.where(is_last, zeros_row, -local_k)
        else:
            upper_row = -local_k
            right_term = zeros_row
        source = take_row(right_side, position, dim)
        divisor = diag_row - lower_row * carried_upper
        carried_upper = upper_row / divisor
        carried_terms = tuple(
            (
                (term_value - lower_row * earlier) / divisor
                for term_value, earlier in zip((source, left_term, right_term), carried_terms)
            )
        )
        upper_list.append(carried_upper)
        terms_list.append(carried_terms)
    behind = (zeros_row, zeros_row, zeros_row)
    solved = [None] * length
    for position in range(length - 1, -1, -1):
        behind = tuple((d - upper_list[position] * x for d, x in zip(terms_list[position], behind)))
        solved[position] = behind
    plain_part = jnp.stack([entry_row[0] for entry_row in solved], axis=dim)
    spike_left = jnp.stack([entry_row[1] for entry_row in solved], axis=dim)
    spike_right = jnp.stack([entry_row[2] for entry_row in solved], axis=dim)
    blocks = jnp.stack(
        [
            zeros_row,
            solved[0][1],
            zeros_row,
            solved[-1][1],
            solved[0][2],
            zeros_row,
            solved[-1][2],
            zeros_row,
            solved[0][0],
            solved[-1][0],
        ]
    )
    return (plain_part, spike_left, spike_right, blocks)


def mat_mul(p, q):
    return (
        p[0] * q[0] + p[1] * q[2],
        p[0] * q[1] + p[1] * q[3],
        p[2] * q[0] + p[3] * q[2],
        p[2] * q[1] + p[3] * q[3],
    )


def mat_vec(p, v):
    return (p[0] * v[0] + p[1] * v[1], p[2] * v[0] + p[3] * v[1])


def combine_rows(blocks, below_rows, above_rows):
    own_a = (blocks[0], blocks[1], blocks[2], blocks[3])
    own_c = (blocks[4], blocks[5], blocks[6], blocks[7])
    own_y = (blocks[8], blocks[9])
    low_a = (below_rows[0], below_rows[1], below_rows[2], below_rows[3])
    low_c = (below_rows[4], below_rows[5], below_rows[6], below_rows[7])
    low_y = (below_rows[8], below_rows[9])
    up_a = (above_rows[0], above_rows[1], above_rows[2], above_rows[3])
    up_c = (above_rows[4], above_rows[5], above_rows[6], above_rows[7])
    up_y = (above_rows[8], above_rows[9])
    a_times_c = mat_mul(own_a, low_c)
    c_times_a = mat_mul(own_c, up_a)
    pivot_mat = (
        1.0 - a_times_c[0] - c_times_a[0],
        -a_times_c[1] - c_times_a[1],
        -a_times_c[2] - c_times_a[2],
        1.0 - a_times_c[3] - c_times_a[3],
    )
    determinant = pivot_mat[0] * pivot_mat[3] - pivot_mat[1] * pivot_mat[2]
    inverse_mat = (
        pivot_mat[3] / determinant,
        -pivot_mat[1] / determinant,
        -pivot_mat[2] / determinant,
        pivot_mat[0] / determinant,
    )
    new_a = mat_mul(inverse_mat, mat_mul(own_a, low_a))
    new_c = mat_mul(inverse_mat, mat_mul(own_c, up_c))
    a_times_y = mat_vec(own_a, low_y)
    c_times_y = mat_vec(own_c, up_y)
    new_y = mat_vec(
        inverse_mat,
        (own_y[0] - a_times_y[0] - c_times_y[0], own_y[1] - a_times_y[1] - c_times_y[1]),
    )
    return jnp.stack(
        [
            -new_a[0],
            -new_a[1],
            -new_a[2],
            -new_a[3],
            -new_c[0],
            -new_c[1],
            -new_c[2],
            -new_c[3],
            new_y[0],
            new_y[1],
        ]
    )


def interface_doubling(blocks, count_dev, fetch_pair):
    reach_dev = 1
    while reach_dev < count_dev:
        below_rows, above_rows = fetch_pair(blocks, blocks, reach_dev)
        blocks = combine_rows(blocks, below_rows, above_rows)
        reach_dev = reach_dev * 2
    return fetch_pair(blocks[9], blocks[8], 1)


def interface_gathered(collected, dev_index):
    blocks = jnp.moveaxis(collected, 0, 1)
    count_dev = blocks.shape[1]
    reach_dev = 1
    while reach_dev < count_dev:
        pad_rows = jnp.zeros_like(blocks[:, :reach_dev])
        below_rows = jnp.concatenate([pad_rows, blocks[:, :-reach_dev]], axis=1)
        above_rows = jnp.concatenate([blocks[:, reach_dev:], pad_rows], axis=1)
        blocks = combine_rows(blocks, below_rows, above_rows)
        reach_dev = reach_dev * 2
    first_values = blocks[8]
    last_values = blocks[9]
    left_value = jnp.where(
        dev_index > 0,
        lax.dynamic_index_in_dim(last_values, jnp.maximum(dev_index - 1, 0), 0, keepdims=False),
        0.0,
    )
    right_value = jnp.where(
        dev_index < count_dev - 1,
        lax.dynamic_index_in_dim(
            first_values, jnp.minimum(dev_index + 1, count_dev - 1), 0, keepdims=False
        ),
        0.0,
    )
    return (left_value, right_value)


def y_fetch(low_part, high_part, reach_dev):
    return (from_behind(low_part, "gy", reach_dev), from_behind(high_part, "gy", -reach_dev))


def solve_along_x(coupling, right_side):
    dev_index = lax.axis_index("gx")
    is_first = dev_index == 0
    is_last = dev_index == lax.axis_size("gx") - 1
    plain_part, spike_left, spike_right, blocks = local_sweeps(
        coupling, right_side, 0, is_first, is_last
    )
    collected = lax.all_gather(blocks[None], "gx", axis=0, tiled=True)
    left_value, right_value = interface_gathered(collected, dev_index)
    return plain_part - spike_left * left_value[None] - spike_right * right_value[None]


def solve_along_y(coupling, right_side):
    dev_index = lax.axis_index("gy")
    is_first = dev_index == 0
    is_last = dev_index == lax.axis_size("gy") - 1
    plain_part, spike_left, spike_right, blocks = local_sweeps(
        coupling, right_side, 1, is_first, is_last
    )
    left_value, right_value = interface_doubling(blocks, lax.axis_size("gy"), y_fetch)
    return plain_part - spike_left * left_value[:, None] - spike_right * right_value[:, None]


def local(fields, region, eps_table):
    inv_eps = lookup_scale(region, eps_table)
    plane_coef = plane_ratio * inv_eps
    depth_coef = depth_ratio * inv_eps
    coupling = plane_ratio * plane_coef
    widened = extend(fields)
    ex_wide = widened[0]
    ey_wide = widened[1]
    ez_wide = widened[2]
    hx_wide = widened[3]
    hy_wide = widened[4]
    hz_wide = widened[5]
    partial_hz = hz_wide - plane_ratio * roll_next(ey_wide, 0)
    partial_hy = hy_wide - depth_ratio * depth_next(ex_wide)
    ey_one = (
        crop_rim(ey_wide)
        + depth_coef * depth_prev(crop_rim(hx_wide))
        - plane_coef * crop_rim(roll_prev(hz_wide, 0))
    )
    rhs_ex = (
        crop_rim(ex_wide)
        + plane_coef * crop_rim(roll_prev(partial_hz, 1))
        - depth_coef * depth_prev(crop_rim(hy_wide))
    )
    rhs_ez = (
        crop_rim(ez_wide)
        + plane_coef * crop_rim(roll_prev(partial_hy, 0))
        - plane_coef * crop_rim(roll_prev(hx_wide, 1))
    )
    ex_one = solve_along_y(coupling, rhs_ex)
    ez_one = solve_along_x(coupling, rhs_ez)
    pair_wide = extend(jnp.stack([ex_one, ez_one]))
    hz_one = crop_rim(partial_hz) + plane_ratio * crop_rim(roll_next(pair_wide[0], 1))
    hy_one = crop_rim(partial_hy) + plane_ratio * crop_rim(roll_next(pair_wide[1], 0))
    hx_one = (
        crop_rim(hx_wide)
        - plane_ratio * crop_rim(roll_next(pair_wide[1], 1))
        + depth_ratio * depth_next(ey_one)
    )
    widened = extend(jnp.stack([ex_one, ey_one, ez_one, hx_one, hy_one, hz_one]))
    ex_wide = widened[0]
    ey_wide = widened[1]
    ez_wide = widened[2]
    hx_wide = widened[3]
    hy_wide = widened[4]
    hz_wide = widened[5]
    ex_two = (
        crop_rim(ex_wide)
        + plane_coef * crop_rim(roll_prev(hz_wide, 1))
        - depth_coef * depth_prev(crop_rim(hy_wide))
    )
    partial_z = hz_wide + plane_ratio * roll_next(ex_wide, 1)
    partial_x = hx_wide + depth_ratio * depth_next(ey_wide)
    rhs_ey = (
        crop_rim(ey_wide)
        + depth_coef * depth_prev(crop_rim(hx_wide))
        - plane_coef * crop_rim(roll_prev(partial_z, 0))
    )
    rhs_ez = (
        crop_rim(ez_wide)
        + plane_coef * crop_rim(roll_prev(hy_wide, 0))
        - plane_coef * crop_rim(roll_prev(partial_x, 1))
    )
    ey_two = solve_along_x(coupling, rhs_ey)
    ez_two = solve_along_y(coupling, rhs_ez)
    pair_wide = extend(jnp.stack([ey_two, ez_two]))
    hz_two = crop_rim(partial_z) - plane_ratio * crop_rim(roll_next(pair_wide[0], 0))
    hx_two = crop_rim(partial_x) - plane_ratio * crop_rim(roll_next(pair_wide[1], 1))
    hy_two = (
        crop_rim(hy_wide)
        - depth_ratio * depth_next(ex_two)
        + plane_ratio * crop_rim(roll_next(pair_wide[1], 0))
    )
    return jnp.stack([ex_two, ey_two, ez_two, hx_two, hy_two, hz_two])


def solution(mesh):
    return jax.shard_map(
        local,
        mesh=mesh,
        in_specs=(P(None, "gx", "gy", None), P("gx", "gy", None), P()),
        out_specs=P(None, "gx", "gy", None),
        check_vma=False,
    )
```

profile of v0, /device:TPU:3, one launch (start us, length us, event | category | flops | bytes accessed | tf_op | source)
XLA Modules:
  0.0 253.8 jit_solution(16521671371981706777)
XLA Ops:
  7.5 3.7 %collective-permute-start = (f32[6,1,32,128]{3,2,1,0:T(8,128)S(1)}, f32[6,1,32,128]{3,2,1,0:T(8,128)S(1)}, u32[]{:S(2)}, u32[]{:S(2)}) collective-permute-start(f32[6,1,32,128]{3,2,1,0:T(8,128)S(1)} %get-tuple-element.639), channel_id=1, source_target_pairs={{0,4},{4,8},{8,12},{12,16},{16,20},{20,24},{24,28},{1,5},{5,9},{9,... | collective-permute-start | bytes 294920 | tf_op jit(solution)/shard_map/ppermute | solution.py:18
  11.2 1.9 collective-permute-start.1
  14.4 1.4 select_reduce_fusion
  16.4 1.5 constant_dynamic-update-slice_fusion.1
  18.1 3.2 %collective-permute-start.2 = (f32[6,18,1,128]{3,2,1,0:T(1,128)S(1)}, f32[6,18,1,128]{3,2,1,0:T(1,128)S(1)}, u32[]{:S(2)}, u32[]{:S(2)}) collective-permute-start(f32[6,18,1,128]{3,2,1,0:T(1,128)S(1)} %get-tuple-element.634), channel_id=1, source_target_pairs={{0,1},{1,2},{2,3},{4,5},{5,6},{6,7},{8,9},{9,10},{10,11},{12,13},{... | collective-permute-start | bytes 165896 | tf_op jit(solution)/shard_map/ppermute | solution.py:18
  23.2 3.0 %collective-permute-done.3 = f32[6,18,1,128]{3,2,1,0:T(1,128)S(1)} collective-permute-done((f32[6,18,1,128]{3,2,1,0:T(1,128)S(1)}, f32[6,18,1,128]{3,2,1,0:T(1,128)S(1)}, u32[]{:S(2)}, u32[]{:S(2)}) %collective-permute-start.3) | collective-permute-done | bytes 55328 | tf_op jit(solution)/shard_map/ppermute | solution.py:20
  32.5 1.6 subtract_divide_fusion.137
  34.1 1.3 negate_multiply_fusion
  36.1 1.5 constant_dynamic-update-slice_fusion.289
  39.4 1.5 constant_dynamic-update-slice_fusion.286
  43.3 1.5 constant_dynamic-update-slice_fusion.68
  46.0 3.2 %collective-permute-start.4 = (f32[10,16,128]{2,1,0:T(8,128)}, f32[10,16,128]{2,1,0:T(8,128)S(1)}, u32[]{:S(2)}, u32[]{:S(2)}) collective-permute-start(f32[10,16,128]{2,1,0:T(8,128)} %constant_dynamic-update-slice_fusion.67), channel_id=1, source_target_pairs={{0,1},{1,2},{2,3},{4,5},{5,6},{6,7},{8,9},{9,10},{10,11},{12,13},{... | collective-permute-start | bytes 245768 | tf_op jit(solution)/shard_map/ppermute | solution.py:30
  50.5 1.8 multiply_subtract_fusion.148
  52.3 1.8 constant_dynamic-update-slice_fusion.66
  55.3 1.5 multiply_subtract_fusion.43
  57.6 1.7 constant_dynamic-update-slice_fusion.227
  60.6 1.5 constant_dynamic-update-slice_fusion.224
  96.5 5.0 %collective-permute-start.6 = (f32[10,16,128]{2,1,0:T(8,128)S(1)}, f32[10,16,128]{2,1,0:T(8,128)S(1)}, u32[]{:S(2)}, u32[]{:S(2)}) collective-permute-start(f32[10,16,128]{2,1,0:T(8,128)S(1)} %constant_dynamic-update-slice_fusion.77), channel_id=1, source_target_pairs={{0,2},{1,3},{4,6},{5,7},{8,10},{9,11},{12,14},{13,15},{16,18},{17,... | collective-permute-start | bytes 245768 | tf_op jit(solution)/shard_map/ppermute | solution.py:30
  104.4 3.9 %collective-permute-done.7 = f32[10,16,128]{2,1,0:T(8,128)S(1)} collective-permute-done((f32[10,16,128]{2,1,0:T(8,128)S(1)}, f32[10,16,128]{2,1,0:T(8,128)S(1)}, u32[]{:S(2)}, u32[]{:S(2)}) %collective-permute-start.7) | collective-permute-done | bytes 81952 | tf_op jit(solution)/shard_map/ppermute | solution.py:30
  108.3 1.3 collective-permute-start.9
  109.6 4.2 %collective-permute-start.8 = (f32[16,128]{1,0:T(8,128)S(1)}, f32[16,128]{1,0:T(8,128)S(1)}, u32[]{:S(2)}, u32[]{:S(2)}) collective-permute-start(f32[16,128]{1,0:T(8,128)S(1)} %get-tuple-element.422), channel_id=1, source_target_pairs={{0,1},{1,2},{2,3},{4,5},{5,6},{6,7},{8,9},{9,10},{10,11},{12,13},{... | collective-permute-start | bytes 24584 | tf_op jit(solution)/shard_map/ppermute | solution.py:30
  115.7 1.4 copy.1059
  124.0 8.8 %collective-permute-start.10 = (f32[2,1,32,128]{3,1,2,0:T(1,128)S(1)}, f32[2,1,32,128]{3,1,2,0:T(1,128)S(1)}, u32[]{:S(2)}, u32[]{:S(2)}) collective-permute-start(f32[2,1,32,128]{3,1,2,0:T(1,128)S(1)} %get-tuple-element.678), channel_id=1, source_target_pairs={{0,4},{4,8},{8,12},{12,16},{16,20},{20,24},{24,28},{1,5},{5,9},{9,... | collective-permute-start | bytes 98312 | tf_op jit(solution)/shard_map/ppermute | solution.py:18
  132.8 1.9 collective-permute-start.11
  134.8 4.2 %collective-permute-done.11 = f32[2,1,32,128]{3,1,2,0:T(1,128)S(1)} collective-permute-done((f32[2,1,32,128]{3,1,2,0:T(1,128)S(1)}, f32[2,1,32,128]{3,1,2,0:T(1,128)S(1)}, u32[]{:S(2)}, u32[]{:S(2)}) %collective-permute-start.11) | collective-permute-done | bytes 32800 | tf_op jit(solution)/shard_map/ppermute | solution.py:20
  139.0 3.9 %collective-permute-start.12 = (f32[2,18,1,128]{3,1,2,0:T(8,128)S(1)}, f32[2,18,1,128]{3,1,2,0:T(8,128)S(1)}, u32[]{:S(2)}, u32[]{:S(2)}) collective-permute-start(f32[2,18,1,128]{3,1,2,0:T(8,128)S(1)} %get-tuple-element.674), channel_id=1, source_target_pairs={{0,1},{1,2},{2,3},{4,5},{5,6},{6,7},{8,9},{9,10},{10,11},{12,13},{... | collective-permute-start | bytes 55304 | tf_op jit(solution)/shard_map/ppermute | solution.py:18
  145.0 2.4 collective-permute-done.13
  149.2 3.3 %collective-permute-start.14 = (f32[6,1,32,128]{3,2,1,0:T(8,128)S(1)}, f32[6,1,32,128]{3,2,1,0:T(8,128)S(1)}, u32[]{:S(2)}, u32[]{:S(2)}) collective-permute-start(f32[6,1,32,128]{3,2,1,0:T(8,128)S(1)} %get-tuple-element.636), channel_id=1, source_target_pairs={{0,4},{4,8},{8,12},{12,16},{16,20},{20,24},{24,28},{1,5},{5,9},{9,... | collective-permute-start | bytes 294920 | tf_op jit(solution)/shard_map/ppermute | solution.py:18
  152.5 1.9 collective-permute-start.15
  155.1 4.3 %collective-permute-done.15 = f32[6,1,32,128]{3,2,1,0:T(8,128)S(1)} collective-permute-done((f32[6,1,32,128]{3,2,1,0:T(8,128)S(1)}, f32[6,1,32,128]{3,2,1,0:T(8,128)S(1)}, u32[]{:S(2)}, u32[]{:S(2)}) %collective-permute-start.15) | collective-permute-done | bytes 98336 | tf_op jit(solution)/shard_map/ppermute | solution.py:20
  159.4 1.6 collective-permute-start.16
  163.0 3.0 %collective-permute-done.17 = f32[6,18,1,128]{3,2,1,0:T(1,128)S(1)} collective-permute-done((f32[6,18,1,128]{3,2,1,0:T(1,128)S(1)}, f32[6,18,1,128]{3,2,1,0:T(1,128)S(1)}, u32[]{:S(2)}, u32[]{:S(2)}) %collective-permute-start.17) | collective-permute-done | bytes 55328 | tf_op jit(solution)/shard_map/ppermute | solution.py:20
  170.7 1.7 constant_dynamic-update-slice_fusion.282
  173.0 1.9 collective-permute-start.18
  174.9 1.5 collective-permute-start.19
  177.9 1.4 fusion.696
  191.3 1.5 constant_dynamic-update-slice_fusion.220
  198.2 3.7 %collective-permute-start.20 = (f32[10,16,128]{2,1,0:T(8,128)S(1)}, f32[10,16,128]{2,1,0:T(8,128)S(1)}, u32[]{:S(2)}, u32[]{:S(2)}) collective-permute-start(f32[10,16,128]{2,1,0:T(8,128)S(1)} %constant_dynamic-update-slice_fusion.291), channel_id=1, source_target_pairs={{0,2},{1,3},{4,6},{5,7},{8,10},{9,11},{12,14},{13,15},{16,18},{17,... | collective-permute-start | bytes 245768 | tf_op jit(solution)/shard_map/ppermute | solution.py:30
  204.8 4.0 %collective-permute-done.21 = f32[10,16,128]{2,1,0:T(8,128)S(1)} collective-permute-done((f32[10,16,128]{2,1,0:T(8,128)S(1)}, f32[10,16,128]{2,1,0:T(8,128)S(1)}, u32[]{:S(2)}, u32[]{:S(2)}) %collective-permute-start.21) | collective-permute-done | bytes 81952 | tf_op jit(solution)/shard_map/ppermute | solution.py:30
  210.2 4.0 %collective-permute-start.22 = (f32[16,128]{1,0:T(8,128)S(1)}, f32[16,128]{1,0:T(8,128)S(1)}, u32[]{:S(2)}, u32[]{:S(2)}) collective-permute-start(f32[16,128]{1,0:T(8,128)S(1)} %get-tuple-element.5), channel_id=1, source_target_pairs={{0,1},{1,2},{2,3},{4,5},{5,6},{6,7},{8,9},{9,10},{10,11},{12,13},{... | collective-permute-start | bytes 24584 | tf_op jit(solution)/shard_map/ppermute | solution.py:30
  215.0 2.8 %all-gather.7.cloned.1.call-done = f32[80,32,128]{2,1,0:T(8,128)} async-done(((f32[10,32,128]{2,1,0:T(8,128)}), f32[80,32,128]{2,1,0:T(8,128)}) %all-gather.7.cloned.1.call-update) | async-done | bytes 1310736 | tf_op jit(solution)/shard_map/all_gather | solution.py:240
  217.8 1.4 copy.1058
  224.7 1.7 constant_dynamic-update-slice_fusion.305
  226.7 3.2 %collective-permute-start.24 = (f32[2,1,32,128]{3,1,2,0:T(1,128)S(1)}, f32[2,1,32,128]{3,1,2,0:T(1,128)S(1)}, u32[]{:S(2)}, u32[]{:S(2)}) collective-permute-start(f32[2,1,32,128]{3,1,2,0:T(1,128)S(1)} %get-tuple-element.676), channel_id=1, source_target_pairs={{0,4},{4,8},{8,12},{12,16},{16,20},{20,24},{24,28},{1,5},{5,9},{9,... | collective-permute-start | bytes 98312 | tf_op jit(solution)/shard_map/ppermute | solution.py:18
  229.9 1.9 collective-permute-start.25
  231.9 4.1 %collective-permute-done.25 = f32[2,1,32,128]{3,1,2,0:T(1,128)S(1)} collective-permute-done((f32[2,1,32,128]{3,1,2,0:T(1,128)S(1)}, f32[2,1,32,128]{3,1,2,0:T(1,128)S(1)}, u32[]{:S(2)}, u32[]{:S(2)}) %collective-permute-start.25) | collective-permute-done | bytes 32800 | tf_op jit(solution)/shard_map/ppermute | solution.py:20
  236.0 3.3 %collective-permute-start.26 = (f32[2,18,1,128]{3,1,2,0:T(8,128)S(1)}, f32[2,18,1,128]{3,1,2,0:T(8,128)S(1)}, u32[]{:S(2)}, u32[]{:S(2)}) collective-permute-start(f32[2,18,1,128]{3,1,2,0:T(8,128)S(1)} %get-tuple-element.672), channel_id=1, source_target_pairs={{0,1},{1,2},{2,3},{4,5},{5,6},{6,7},{8,9},{9,10},{10,11},{12,13},{... | collective-permute-start | bytes 55304 | tf_op jit(solution)/shard_map/ppermute | solution.py:18
  241.4 2.5 collective-permute-done.27
  (819 shorter events, 110.0 us)
Async XLA Ops:
  6.5 109.1 %all-gather.5.cloned.1.call-start = ((), (), s32[]{:S(2)}) async-start(), calls=%async_computation | async-start | bytes 1474560 | tf_op jit(solution)/shard_map/all_gather | solution.py:240
  7.5 8.9 %collective-permute-start = (f32[6,1,32,128]{3,2,1,0:T(8,128)S(1)}, f32[6,1,32,128]{3,2,1,0:T(8,128)S(1)}, u32[]{:S(2)}, u32[]{:S(2)}) collective-permute-start(f32[6,1,32,128]{3,2,1,0:T(8,128)S(1)} %get-tuple-element.639), channel_id=1, source_target_pairs={{0,4},{4,8},{8,12},{12,16},{16,20},{20,24},{24,28},{1,5},{5,9},{9,... | collective-permute-start | bytes 294920 | tf_op jit(solution)/shard_map/ppermute | solution.py:18
  11.2 6.8 %collective-permute-start.1 = (f32[6,1,32,128]{3,2,1,0:T(8,128)S(1)}, f32[6,1,32,128]{3,2,1,0:T(8,128)S(1)}, u32[]{:S(2)}, u32[]{:S(2)}) collective-permute-start(f32[6,1,32,128]{3,2,1,0:T(8,128)S(1)} %get-tuple-element.638), channel_id=1, source_target_pairs={{4,0},{8,4},{12,8},{16,12},{20,16},{24,20},{28,24},{5,1},{9,5},{13... | collective-permute-start | bytes 294920 | tf_op jit(solution)/shard_map/ppermute | solution.py:20
  18.1 5.1 %collective-permute-start.2 = (f32[6,18,1,128]{3,2,1,0:T(1,128)S(1)}, f32[6,18,1,128]{3,2,1,0:T(1,128)S(1)}, u32[]{:S(2)}, u32[]{:S(2)}) collective-permute-start(f32[6,18,1,128]{3,2,1,0:T(1,128)S(1)} %get-tuple-element.634), channel_id=1, source_target_pairs={{0,1},{1,2},{2,3},{4,5},{5,6},{6,7},{8,9},{9,10},{10,11},{12,13},{... | collective-permute-start | bytes 165896 | tf_op jit(solution)/shard_map/ppermute | solution.py:18
  21.3 4.9 %collective-permute-start.3 = (f32[6,18,1,128]{3,2,1,0:T(1,128)S(1)}, f32[6,18,1,128]{3,2,1,0:T(1,128)S(1)}, u32[]{:S(2)}, u32[]{:S(2)}) collective-permute-start(f32[6,18,1,128]{3,2,1,0:T(1,128)S(1)} %get-tuple-element.635), channel_id=1, source_target_pairs={{1,0},{2,1},{3,2},{5,4},{6,5},{7,6},{9,8},{10,9},{11,10},{13,12},{... | collective-permute-start | bytes 165896 | tf_op jit(solution)/shard_map/ppermute | solution.py:20
  29.9 73.0 %copy-start.12 = (f32[16,1,128]{2,1,0:T(1,128)}, f32[16,1,128]{2,1,0:T(1,128)S(1)}, u32[]{:S(2)}) copy-start(f32[16,1,128]{2,1,0:T(1,128)S(1)} %get-tuple-element.753) | copy-start | bytes 24580
  29.9 73.0 %copy-start.14 = (f32[16,1,128]{2,1,0:T(1,128)}, f32[16,1,128]{2,1,0:T(1,128)S(1)}, u32[]{:S(2)}) copy-start(f32[16,1,128]{2,1,0:T(1,128)S(1)} %get-tuple-element.755) | copy-start | bytes 24580
  29.9 73.0 %copy-start.16 = (f32[16,1,128]{2,1,0:T(1,128)}, f32[16,1,128]{2,1,0:T(1,128)S(1)}, u32[]{:S(2)}) copy-start(f32[16,1,128]{2,1,0:T(1,128)S(1)} %get-tuple-element.756) | copy-start | bytes 24580
  29.9 73.0 %copy-start.18 = (f32[16,1,128]{2,1,0:T(1,128)}, f32[16,1,128]{2,1,0:T(1,128)S(1)}, u32[]{:S(2)}) copy-start(f32[16,1,128]{2,1,0:T(1,128)S(1)} %get-tuple-element.757) | copy-start | bytes 24580
  29.9 73.0 %copy-start.20 = (f32[16,1,128]{2,1,0:T(1,128)}, f32[16,1,128]{2,1,0:T(1,128)S(1)}, u32[]{:S(2)}) copy-start(f32[16,1,128]{2,1,0:T(1,128)S(1)} %get-tuple-element.759) | copy-start | bytes 24580
  29.9 73.0 %copy-start.34 = (f32[16,1,128]{2,1,0:T(1,128)}, f32[16,1,128]{2,1,0:T(1,128)S(1)}, u32[]{:S(2)}) copy-start(f32[16,1,128]{2,1,0:T(1,128)S(1)} %get-tuple-element.741) | copy-start | bytes 24580
  29.9 73.0 %copy-start.36 = (f32[16,1,128]{2,1,0:T(1,128)}, f32[16,1,128]{2,1,0:T(1,128)S(1)}, u32[]{:S(2)}) copy-start(f32[16,1,128]{2,1,0:T(1,128)S(1)} %get-tuple-element.745) | copy-start | bytes 24580
  29.9 73.0 %copy-start.38 = (f32[16,1,128]{2,1,0:T(1,128)}, f32[16,1,128]{2,1,0:T(1,128)S(1)}, u32[]{:S(2)}) copy-start(f32[16,1,128]{2,1,0:T(1,128)S(1)} %get-tuple-element.747) | copy-start | bytes 24580
  29.9 73.0 %copy-start.40 = (f32[16,1,128]{2,1,0:T(1,128)}, f32[16,1,128]{2,1,0:T(1,128)S(1)}, u32[]{:S(2)}) copy-start(f32[16,1,128]{2,1,0:T(1,128)S(1)} %get-tuple-element.749) | copy-start | bytes 24580
  29.9 73.0 %copy-start.42 = (f32[16,1,128]{2,1,0:T(1,128)}, f32[16,1,128]{2,1,0:T(1,128)S(1)}, u32[]{:S(2)}) copy-start(f32[16,1,128]{2,1,0:T(1,128)S(1)} %get-tuple-element.751) | copy-start | bytes 24580
  30.0 73.0 %copy-start.44 = (f32[16,1,128]{2,1,0:T(1,128)}, f32[16,1,128]{2,1,0:T(1,128)S(1)}, u32[]{:S(2)}) copy-start(f32[16,1,128]{2,1,0:T(1,128)S(1)} %get-tuple-element.742) | copy-start | bytes 24580
  30.0 73.0 %copy-start.54 = (f32[16,1,128]{2,1,0:T(1,128)}, f32[16,1,128]{2,1,0:T(1,128)S(1)}, u32[]{:S(2)}) copy-start(f32[16,1,128]{2,1,0:T(1,128)S(1)} %get-tuple-element.743) | copy-start | bytes 24580
  30.1 72.9 %copy-start.22 = (f32[16,1,128]{2,1,0:T(1,128)}, f32[16,1,128]{2,1,0:T(1,128)S(1)}, u32[]{:S(2)}) copy-start(f32[16,1,128]{2,1,0:T(1,128)S(1)} %get-tuple-element.762) | copy-start | bytes 24580
  30.1 72.9 %copy-start.24 = (f32[16,1,128]{2,1,0:T(1,128)}, f32[16,1,128]{2,1,0:T(1,128)S(1)}, u32[]{:S(2)}) copy-start(f32[16,1,128]{2,1,0:T(1,128)S(1)} %get-tuple-element.764) | copy-start | bytes 24580
  30.1 72.9 %copy-start.26 = (f32[16,1,128]{2,1,0:T(1,128)}, f32[16,1,128]{2,1,0:T(1,128)S(1)}, u32[]{:S(2)}) copy-start(f32[16,1,128]{2,1,0:T(1,128)S(1)} %get-tuple-element.765) | copy-start | bytes 24580
  30.1 72.9 %copy-start.28 = (f32[16,1,128]{2,1,0:T(1,128)}, f32[16,1,128]{2,1,0:T(1,128)S(1)}, u32[]{:S(2)}) copy-start(f32[16,1,128]{2,1,0:T(1,128)S(1)} %get-tuple-element.766) | copy-start | bytes 24580
  30.1 72.9 %copy-start.30 = (f32[16,1,128]{2,1,0:T(1,128)}, f32[16,1,128]{2,1,0:T(1,128)S(1)}, u32[]{:S(2)}) copy-start(f32[16,1,128]{2,1,0:T(1,128)S(1)} %get-tuple-element.768) | copy-start | bytes 24580
  30.1 72.9 %copy-start.32 = (f32[16,1,128]{2,1,0:T(1,128)}, f32[16,1,128]{2,1,0:T(1,128)S(1)}, u32[]{:S(2)}) copy-start(f32[16,1,128]{2,1,0:T(1,128)S(1)} %get-tuple-element.770) | copy-start | bytes 24580
  46.0 49.7 %collective-permute-start.4 = (f32[10,16,128]{2,1,0:T(8,128)}, f32[10,16,128]{2,1,0:T(8,128)S(1)}, u32[]{:S(2)}, u32[]{:S(2)}) collective-permute-start(f32[10,16,128]{2,1,0:T(8,128)} %constant_dynamic-update-slice_fusion.67), channel_id=1, source_target_pairs={{0,1},{1,2},{2,3},{4,5},{5,6},{6,7},{8,9},{9,10},{10,11},{12,13},{... | collective-permute-start | bytes 245768 | tf_op jit(solution)/shard_map/ppermute | solution.py:30
  49.2 46.5 %collective-permute-start.5 = (f32[10,16,128]{2,1,0:T(8,128)}, f32[10,16,128]{2,1,0:T(8,128)S(1)}, u32[]{:S(2)}, u32[]{:S(2)}) collective-permute-start(f32[10,16,128]{2,1,0:T(8,128)} %constant_dynamic-update-slice_fusion.67), channel_id=1, source_target_pairs={{1,0},{2,1},{3,2},{5,4},{6,5},{7,6},{9,8},{10,9},{11,10},{13,12},{... | collective-permute-start | bytes 245768 | tf_op jit(solution)/shard_map/ppermute | solution.py:30
  79.6 138.3 %all-gather.7.cloned.1.call-start = ((), (), s32[]{:S(2)}) async-start(), calls=%async_computation.1 | async-start | bytes 1474560 | tf_op jit(solution)/shard_map/all_gather | solution.py:240
  96.5 7.8 %collective-permute-start.6 = (f32[10,16,128]{2,1,0:T(8,128)S(1)}, f32[10,16,128]{2,1,0:T(8,128)S(1)}, u32[]{:S(2)}, u32[]{:S(2)}) collective-permute-start(f32[10,16,128]{2,1,0:T(8,128)S(1)} %constant_dynamic-update-slice_fusion.77), channel_id=1, source_target_pairs={{0,2},{1,3},{4,6},{5,7},{8,10},{9,11},{12,14},{13,15},{16,18},{17,... | collective-permute-start | bytes 245768 | tf_op jit(solution)/shard_map/ppermute | solution.py:30
  101.6 6.7 %collective-permute-start.7 = (f32[10,16,128]{2,1,0:T(8,128)S(1)}, f32[10,16,128]{2,1,0:T(8,128)S(1)}, u32[]{:S(2)}, u32[]{:S(2)}) collective-permute-start(f32[10,16,128]{2,1,0:T(8,128)S(1)} %constant_dynamic-update-slice_fusion.77), channel_id=1, source_target_pairs={{2,0},{3,1},{6,4},{7,5},{10,8},{11,9},{14,12},{15,13},{18,16},{19,... | collective-permute-start | bytes 245768 | tf_op jit(solution)/shard_map/ppermute | solution.py:30
  108.3 5.5 %collective-permute-start.9 = (f32[16,128]{1,0:T(8,128)S(1)}, f32[16,128]{1,0:T(8,128)S(1)}, u32[]{:S(2)}, u32[]{:S(2)}) collective-permute-start(f32[16,128]{1,0:T(8,128)S(1)} %multiply_add_fusion.47), channel_id=1, source_target_pairs={{1,0},{2,1},{3,2},{5,4},{6,5},{7,6},{9,8},{10,9},{11,10},{13,12},{... | collective-permute-start | bytes 24584 | tf_op jit(solution)/shard_map/ppermute | solution.py:30
  109.6 4.8 %collective-permute-start.8 = (f32[16,128]{1,0:T(8,128)S(1)}, f32[16,128]{1,0:T(8,128)S(1)}, u32[]{:S(2)}, u32[]{:S(2)}) collective-permute-start(f32[16,128]{1,0:T(8,128)S(1)} %get-tuple-element.422), channel_id=1, source_target_pairs={{0,1},{1,2},{2,3},{4,5},{5,6},{6,7},{8,9},{9,10},{10,11},{12,13},{... | collective-permute-start | bytes 24584 | tf_op jit(solution)/shard_map/ppermute | solution.py:30
  124.0 10.7 %collective-permute-start.10 = (f32[2,1,32,128]{3,1,2,0:T(1,128)S(1)}, f32[2,1,32,128]{3,1,2,0:T(1,128)S(1)}, u32[]{:S(2)}, u32[]{:S(2)}) collective-permute-start(f32[2,1,32,128]{3,1,2,0:T(1,128)S(1)} %get-tuple-element.678), channel_id=1, source_target_pairs={{0,4},{4,8},{8,12},{12,16},{16,20},{20,24},{24,28},{1,5},{5,9},{9,... | collective-permute-start | bytes 98312 | tf_op jit(solution)/shard_map/ppermute | solution.py:18
  132.8 6.1 %collective-permute-start.11 = (f32[2,1,32,128]{3,1,2,0:T(1,128)S(1)}, f32[2,1,32,128]{3,1,2,0:T(1,128)S(1)}, u32[]{:S(2)}, u32[]{:S(2)}) collective-permute-start(f32[2,1,32,128]{3,1,2,0:T(1,128)S(1)} %get-tuple-element.679), channel_id=1, source_target_pairs={{4,0},{8,4},{12,8},{16,12},{20,16},{24,20},{28,24},{5,1},{9,5},{13... | collective-permute-start | bytes 98312 | tf_op jit(solution)/shard_map/ppermute | solution.py:20
  139.0 6.1 %collective-permute-start.12 = (f32[2,18,1,128]{3,1,2,0:T(8,128)S(1)}, f32[2,18,1,128]{3,1,2,0:T(8,128)S(1)}, u32[]{:S(2)}, u32[]{:S(2)}) collective-permute-start(f32[2,18,1,128]{3,1,2,0:T(8,128)S(1)} %get-tuple-element.674), channel_id=1, source_target_pairs={{0,1},{1,2},{2,3},{4,5},{5,6},{6,7},{8,9},{9,10},{10,11},{12,13},{... | collective-permute-start | bytes 55304 | tf_op jit(solution)/shard_map/ppermute | solution.py:18
  142.9 4.6 %collective-permute-start.13 = (f32[2,18,1,128]{3,1,2,0:T(8,128)S(1)}, f32[2,18,1,128]{3,1,2,0:T(8,128)S(1)}, u32[]{:S(2)}, u32[]{:S(2)}) collective-permute-start(f32[2,18,1,128]{3,1,2,0:T(8,128)S(1)} %get-tuple-element.675), channel_id=1, source_target_pairs={{1,0},{2,1},{3,2},{5,4},{6,5},{7,6},{9,8},{10,9},{11,10},{13,12},{... | collective-permute-start | bytes 55304 | tf_op jit(solution)/shard_map/ppermute | solution.py:20
  149.2 5.9 %collective-permute-start.14 = (f32[6,1,32,128]{3,2,1,0:T(8,128)S(1)}, f32[6,1,32,128]{3,2,1,0:T(8,128)S(1)}, u32[]{:S(2)}, u32[]{:S(2)}) collective-permute-start(f32[6,1,32,128]{3,2,1,0:T(8,128)S(1)} %get-tuple-element.636), channel_id=1, source_target_pairs={{0,4},{4,8},{8,12},{12,16},{16,20},{20,24},{24,28},{1,5},{5,9},{9,... | collective-permute-start | bytes 294920 | tf_op jit(solution)/shard_map/ppermute | solution.py:18
  152.5 6.8 %collective-permute-start.15 = (f32[6,1,32,128]{3,2,1,0:T(8,128)S(1)}, f32[6,1,32,128]{3,2,1,0:T(8,128)S(1)}, u32[]{:S(2)}, u32[]{:S(2)}) collective-permute-start(f32[6,1,32,128]{3,2,1,0:T(8,128)S(1)} %get-tuple-element.637), channel_id=1, source_target_pairs={{4,0},{8,4},{12,8},{16,12},{20,16},{24,20},{28,24},{5,1},{9,5},{13... | collective-permute-start | bytes 294920 | tf_op jit(solution)/shard_map/ppermute | solution.py:20
  159.4 3.6 %collective-permute-start.16 = (f32[6,18,1,128]{3,2,1,0:T(1,128)S(1)}, f32[6,18,1,128]{3,2,1,0:T(1,128)S(1)}, u32[]{:S(2)}, u32[]{:S(2)}) collective-permute-start(f32[6,18,1,128]{3,2,1,0:T(1,128)S(1)} %get-tuple-element.632), channel_id=1, source_target_pairs={{0,1},{1,2},{2,3},{4,5},{5,6},{6,7},{8,9},{9,10},{10,11},{12,13},{... | collective-permute-start | bytes 165896 | tf_op jit(solution)/shard_map/ppermute | solution.py:18
  161.1 4.9 %collective-permute-start.17 = (f32[6,18,1,128]{3,2,1,0:T(1,128)S(1)}, f32[6,18,1,128]{3,2,1,0:T(1,128)S(1)}, u32[]{:S(2)}, u32[]{:S(2)}) collective-permute-start(f32[6,18,1,128]{3,2,1,0:T(1,128)S(1)} %get-tuple-element.633), channel_id=1, source_target_pairs={{1,0},{2,1},{3,2},{5,4},{6,5},{7,6},{9,8},{10,9},{11,10},{13,12},{... | collective-permute-start | bytes 165896 | tf_op jit(solution)/shard_map/ppermute | solution.py:20
  173.0 24.3 %collective-permute-start.18 = (f32[10,16,128]{2,1,0:T(8,128)}, f32[10,16,128]{2,1,0:T(8,128)S(1)}, u32[]{:S(2)}, u32[]{:S(2)}) collective-permute-start(f32[10,16,128]{2,1,0:T(8,128)} %constant_dynamic-update-slice_fusion.281), channel_id=1, source_target_pairs={{0,1},{1,2},{2,3},{4,5},{5,6},{6,7},{8,9},{9,10},{10,11},{12,13},{... | collective-permute-start | bytes 245768 | tf_op jit(solution)/shard_map/ppermute | solution.py:30
  174.9 22.3 %collective-permute-start.19 = (f32[10,16,128]{2,1,0:T(8,128)}, f32[10,16,128]{2,1,0:T(8,128)S(1)}, u32[]{:S(2)}, u32[]{:S(2)}) collective-permute-start(f32[10,16,128]{2,1,0:T(8,128)} %constant_dynamic-update-slice_fusion.281), channel_id=1, source_target_pairs={{1,0},{2,1},{3,2},{5,4},{6,5},{7,6},{9,8},{10,9},{11,10},{13,12},{... | collective-permute-start | bytes 245768 | tf_op jit(solution)/shard_map/ppermute | solution.py:30
  198.2 6.7 %collective-permute-start.20 = (f32[10,16,128]{2,1,0:T(8,128)S(1)}, f32[10,16,128]{2,1,0:T(8,128)S(1)}, u32[]{:S(2)}, u32[]{:S(2)}) collective-permute-start(f32[10,16,128]{2,1,0:T(8,128)S(1)} %constant_dynamic-update-slice_fusion.291), channel_id=1, source_target_pairs={{0,2},{1,3},{4,6},{5,7},{8,10},{9,11},{12,14},{13,15},{16,18},{17,... | collective-permute-start | bytes 245768 | tf_op jit(solution)/shard_map/ppermute | solution.py:30
  201.9 7.0 %collective-permute-start.21 = (f32[10,16,128]{2,1,0:T(8,128)S(1)}, f32[10,16,128]{2,1,0:T(8,128)S(1)}, u32[]{:S(2)}, u32[]{:S(2)}) collective-permute-start(f32[10,16,128]{2,1,0:T(8,128)S(1)} %constant_dynamic-update-slice_fusion.291), channel_id=1, source_target_pairs={{2,0},{3,1},{6,4},{7,5},{10,8},{11,9},{14,12},{15,13},{18,16},{19,... | collective-permute-start | bytes 245768 | tf_op jit(solution)/shard_map/ppermute | solution.py:30
  208.9 5.3 %collective-permute-start.23 = (f32[16,128]{1,0:T(8,128)S(1)}, f32[16,128]{1,0:T(8,128)S(1)}, u32[]{:S(2)}, u32[]{:S(2)}) collective-permute-start(f32[16,128]{1,0:T(8,128)S(1)} %multiply_add_fusion.38), channel_id=1, source_target_pairs={{1,0},{2,1},{3,2},{5,4},{6,5},{7,6},{9,8},{10,9},{11,10},{13,12},{... | collective-permute-start | bytes 24584 | tf_op jit(solution)/shard_map/ppermute | solution.py:30
  210.2 4.8 %collective-permute-start.22 = (f32[16,128]{1,0:T(8,128)S(1)}, f32[16,128]{1,0:T(8,128)S(1)}, u32[]{:S(2)}, u32[]{:S(2)}) collective-permute-start(f32[16,128]{1,0:T(8,128)S(1)} %get-tuple-element.5), channel_id=1, source_target_pairs={{0,1},{1,2},{2,3},{4,5},{5,6},{6,7},{8,9},{9,10},{10,11},{12,13},{... | collective-permute-start | bytes 24584 | tf_op jit(solution)/shard_map/ppermute | solution.py:30
  226.7 5.3 %collective-permute-start.24 = (f32[2,1,32,128]{3,1,2,0:T(1,128)S(1)}, f32[2,1,32,128]{3,1,2,0:T(1,128)S(1)}, u32[]{:S(2)}, u32[]{:S(2)}) collective-permute-start(f32[2,1,32,128]{3,1,2,0:T(1,128)S(1)} %get-tuple-element.676), channel_id=1, source_target_pairs={{0,4},{4,8},{8,12},{12,16},{16,20},{20,24},{24,28},{1,5},{5,9},{9,... | collective-permute-start | bytes 98312 | tf_op jit(solution)/shard_map/ppermute | solution.py:18
  229.9 6.1 %collective-permute-start.25 = (f32[2,1,32,128]{3,1,2,0:T(1,128)S(1)}, f32[2,1,32,128]{3,1,2,0:T(1,128)S(1)}, u32[]{:S(2)}, u32[]{:S(2)}) collective-permute-start(f32[2,1,32,128]{3,1,2,0:T(1,128)S(1)} %get-tuple-element.677), channel_id=1, source_target_pairs={{4,0},{8,4},{12,8},{16,12},{20,16},{24,20},{28,24},{5,1},{9,5},{13... | collective-permute-start | bytes 98312 | tf_op jit(solution)/shard_map/ppermute | solution.py:20
  236.0 5.4 %collective-permute-start.26 = (f32[2,18,1,128]{3,1,2,0:T(8,128)S(1)}, f32[2,18,1,128]{3,1,2,0:T(8,128)S(1)}, u32[]{:S(2)}, u32[]{:S(2)}) collective-permute-start(f32[2,18,1,128]{3,1,2,0:T(8,128)S(1)} %get-tuple-element.672), channel_id=1, source_target_pairs={{0,1},{1,2},{2,3},{4,5},{5,6},{6,7},{8,9},{9,10},{10,11},{12,13},{... | collective-permute-start | bytes 55304 | tf_op jit(solution)/shard_map/ppermute | solution.py:18
  239.3 4.6 %collective-permute-start.27 = (f32[2,18,1,128]{3,1,2,0:T(8,128)S(1)}, f32[2,18,1,128]{3,1,2,0:T(8,128)S(1)}, u32[]{:S(2)}, u32[]{:S(2)}) collective-permute-start(f32[2,18,1,128]{3,1,2,0:T(8,128)S(1)} %get-tuple-element.673), channel_id=1, source_target_pairs={{1,0},{2,1},{3,2},{5,4},{6,5},{7,6},{9,8},{10,9},{11,10},{13,12},{... | collective-permute-start | bytes 55304 | tf_op jit(solution)/shard_map/ppermute | solution.py:20
  (184 other events, 2164.7 us)
Sparse Core Ops, SparseCore 0:
  79.7 27.9 all-gather.4
  193.8 24.0 all-gather.6
where the time goes:
time: 259 us; the launch traced here: 254 us
  other arithmetic  80.8 us (31%)
  starting transfers between devices  73.9 us (29%)
  local copies, waits for them, and re-layouts  45.5 us (18%)
  waiting for transfers between devices  35.5 us (14%)
  between operations  18.1 us (7%)
    unnamed x120, other arithmetic  50.2 us
    unnamed x521, local copies, waits for them, and re-layouts  32.4 us
    ppermute x8, starting transfers between devices, padded(): lax.ppermute(tail, axis, [(i, (i + 1) % count) for i in range(ends)])  31 us
    ppermute x12, starting transfers between devices, from_behind(): return lax.ppermute(block, axis, route)  29.9 us
    ppermute x8, waiting for transfers between devices, padded(): lax.ppermute(head, axis, [((i + 1) % count, i) for i in range(ends)])  23.5 us
    ppermute x8, starting transfers between devices, padded(): lax.ppermute(head, axis, [((i + 1) % count, i) for i in range(ends)])  12.9 us
    ppermute x12, waiting for transfers between devices, from_behind(): return lax.ppermute(block, axis, route)  9.17 us
  transfers between devices with their start and end apart: 30, of which 12 were waited for; matrix products, arithmetic and copies ran while one was open for 30% of the time, Pallas kernels for 0%

commit v1 on v0

v1 whole, which is shorter than its diff:
```python
import functools

import jax
import jax.numpy as jnp
from jax import lax
from jax.experimental import pallas as pl
from jax.experimental.pallas import tpu as pltpu
from jax.sharding import PartitionSpec as P

MESH = pl.DeviceIdType.MESH
EX, EY, EZ, HX, HY, HZ = range(6)


def kernel(
    n, m, nx, ny, nz, labels,
    fields, region, eps, out,
    ce, inv_x, c_x, l_x, r_x, inv_y, c_y, l_y, r_y,
    p_x, p_y, rhs, p1, ey1, ez1, ex1, p2,
    ey_next, hz_prev, hx_prev, hx_send, ez_next, ez_send, v_next, wr_x, wr_y,
    mx_send, mx_recv, gx_one, gx_two, coef_x, sx_send, sx_recv,
    my_send, my_recv, gy_one, gy_two, coef_y, sy_send, sy_recv,
    near_send, near_recv, x_send, x_recv, y_send, y_recv,
):
    gx = lax.axis_index("gx")
    gy = lax.axis_index("gy")

    barrier = pltpu.get_barrier_semaphore()
    for k in range(1, n):
        pl.semaphore_signal(
            barrier, inc=1, device_id={"gx": lax.rem(gx + k, n)}, device_id_type=MESH
        )
    for k in range(1, m):
        pl.semaphore_signal(
            barrier, inc=1, device_id={"gy": lax.rem(gy + k, m)}, device_id_type=MESH
        )

    def plane(i):
        return pl.ds(pl.multiple_of(i * ny, ny), ny)

    def row(j):
        return pl.ds(pl.multiple_of(j * nx, nx), nx)

    def across(j):
        return pl.ds(j, nx, stride=ny)

    lane = lax.broadcasted_iota(jnp.int32, (ny, nz), 1)
    sub = lax.broadcasted_iota(jnp.int32, (ny, nz), 0)
    zero_plane = jnp.zeros((ny, nz), jnp.float32)
    zero_row = jnp.zeros((nx, nz), jnp.float32)

    def f_z(v):
        return jnp.where(lane == nz - 1, 0.0, pltpu.roll(v, nz - 1, 1)) - v

    def b_z(v):
        return v - jnp.where(lane == 0, 0.0, pltpu.roll(v, 1, 1))

    def f_y(v, after):
        return jnp.where(sub == ny - 1, after, pltpu.roll(v, ny - 1, 0)) - v

    def b_y(v, before):
        return v - jnp.where(sub == 0, before, pltpu.roll(v, 1, 0))

    def near(src, dst, slot, device):
        return pltpu.make_async_remote_copy(
            src_ref=src, dst_ref=dst, send_sem=near_send.at[slot],
            recv_sem=near_recv.at[slot], device_id=device, device_id_type=MESH,
        )

    to_left = {"gx": jnp.maximum(gx - 1, 0)}
    to_right = {"gx": jnp.minimum(gx + 1, n - 1)}
    to_low = {"gy": jnp.maximum(gy - 1, 0)}
    to_high = {"gy": jnp.minimum(gy + 1, m - 1)}
    send_ey = near(fields.at[EY, pl.ds(0, ny)], ey_next, 0, to_left)
    send_hz = near(fields.at[HZ, pl.ds((nx - 1) * ny, ny)], hz_prev, 1, to_right)
    send_hx = near(hx_send, hx_prev, 2, to_high)
    send_ez = near(ez_send, ez_next, 3, to_low)
    send_v = near(rhs.at[pl.ds(0, ny)], v_next, 4, to_left)

    has_left = gx > 0
    has_right = gx < n - 1
    has_low = gy > 0
    has_high = gy < m - 1

    def start(cond, copy):
        @pl.when(cond)
        def _():
            copy.start()

    def sent(cond, copy):
        @pl.when(cond)
        def _():
            copy.wait_send()

    def arrived(cond, copy, ref):
        @pl.when(cond)
        def _():
            copy.wait_recv()

        @pl.when(jnp.logical_not(cond))
        def _():
            ref[...] = jnp.zeros(ref.shape, jnp.float32)

    hx_send[...] = fields[HX, across(ny - 1), :]

    def x_copy(kind, k, src, dst):
        target = lax.rem(gx + k, n)
        return pltpu.make_async_remote_copy(
            src_ref=src, dst_ref=dst.at[gx], send_sem=x_send.at[kind, k],
            recv_sem=x_recv.at[kind, gx], device_id={"gx": target}, device_id_type=MESH,
        )

    def y_copy(kind, k, src, dst):
        target = lax.rem(gy + k, m)
        return pltpu.make_async_remote_copy(
            src_ref=src, dst_ref=dst.at[gy], send_sem=y_send.at[kind, k],
            recv_sem=y_recv.at[kind, gy], device_id={"gy": target}, device_id_type=MESH,
        )

    def x_wait(kind, src, dst, j):
        pltpu.make_async_remote_copy(
            src_ref=src, dst_ref=dst.at[j], send_sem=x_send.at[kind, 0],
            recv_sem=x_recv.at[kind, j], device_id={"gx": j}, device_id_type=MESH,
        ).wait_recv()

    def y_wait(kind, src, dst, j):
        pltpu.make_async_remote_copy(
            src_ref=src, dst_ref=dst.at[j], send_sem=y_send.at[kind, 0],
            recv_sem=y_recv.at[kind, j], device_id={"gy": j}, device_id_type=MESH,
        ).wait_recv()

    pl.semaphore_wait(barrier, n + m - 2)
    start(has_left, send_ey)
    start(has_high, send_hx)
    start(has_right, send_hz)

    def pick(label, lowest, width):
        if width == 1:
            return eps[lowest]
        half = width // 2
        return jnp.where(
            (label & half) != 0,
            pick(label, lowest + half, half),
            pick(label, lowest, half),
        )

    def coefficients(i, _):
        s = plane(i)
        label = region[s, :]
        ce[s, :] = 32.0 / pick(label, 0, labels)
        return 0

    lax.fori_loop(0, nx, coefficients, 0)

    def factor(count, load_ce, at, first, zero, inv_ref, c_ref, l_ref, r_ref, send_ref):
        ones = zero + 1.0

        def forward(i, carry):
            c_last, d_last = carry
            kk = 32.0 * load_ce(i)
            inv = 1.0 / (1.0 + (2.0 * kk - kk * c_last))
            c = kk * inv
            d = c * d_last
            s = at(i)
            inv_ref[s, :] = inv
            c_ref[s, :] = c
            l_ref[s, :] = d
            return c, d

        lax.fori_loop(0, count, forward, (zero + jnp.where(first, 1.0, 0.0), ones))

        def backward(t, carry):
            l_after, r_after = carry
            s = at(count - 1 - t)
            c = c_ref[s, :]
            l = l_ref[s, :] + c * l_after
            r = c * r_after
            l_ref[s, :] = l
            r_ref[s, :] = r
            return l, r

        l_first, r_first = lax.fori_loop(0, count, backward, (zero, ones))
        send_ref[0] = l_first
        send_ref[1] = r_ref[at(count - 1), :]
        send_ref[2] = r_first

    factor(nx, lambda i: ce[plane(i), :], plane, gx == 0, zero_plane,
           inv_x, c_x, l_x, r_x, mx_send)
    for k in range(1, n):
        x_copy(0, k, mx_send, mx_recv).start()
    factor(ny, lambda j: ce[across(j), :], row, gy == 0, zero_row,
           inv_y, c_y, l_y, r_y, my_send)
    for k in range(1, m):
        y_copy(0, k, my_send, my_recv).start()

    def backward_sweep(count, at, zero, c_ref, p_ref):
        def body(t, after):
            s = at(count - 1 - t)
            w = p_ref[s, :] + c_ref[s, :] * after
            p_ref[s, :] = w
            return w

        return lax.fori_loop(0, count, body, zero)

    def y_sweep():
        def body(j, last):
            s = row(j)
            d = rhs[across(j), :] * inv_y[s, :] + c_y[s, :] * last
            p_y[s, :] = d
            return d

        last = lax.fori_loop(0, ny, body, zero_row)
        return backward_sweep(ny, row, zero_row, c_y, p_y), last

    arrived(has_low, send_hx, hx_prev)

    def ez_forward(i, carry):
        q_last, d_last = carry
        s = plane(i)
        q = fields[HY, s, :] - 0.5 * f_z(fields[EX, s, :])
        coef = ce[s, :]
        r = fields[EZ, s, :] + coef * (
            (q - q_last) - b_y(fields[HX, s, :], hx_prev[pl.ds(i, 1), :])
        )
        d = r * inv_x[s, :] + c_x[s, :] * d_last
        p_x[s, :] = d
        return q, d

    q_end, ez_last = lax.fori_loop(0, nx, ez_forward, (zero_plane, zero_plane))
    sx_send[0, 0] = backward_sweep(nx, plane, zero_plane, c_x, p_x)
    sx_send[0, 1] = ez_last - q_end * 0.03125
    for k in range(1, n):
        x_copy(1, k, sx_send.at[0], sx_recv.at[0]).start()

    arrived(has_right, send_ey, ey_next)

    def ex_right(i, ey_after):
        i = nx - 1 - i
        s = plane(i)
        ey_here = fields[EY, s, :]
        p = fields[HZ, s, :] - 32.0 * (ey_after - ey_here)
        p1[s, :] = p
        coef = ce[s, :]
        rhs[s, :] = fields[EX, s, :] + coef * (
            b_y(p, 0.0) - 0.015625 * b_z(fields[HY, s, :])
        )
        return ey_here

    lax.fori_loop(0, nx, ex_right, ey_next[...])
    ex_first, ex_last = y_sweep()
    sy_send[0, 0] = ex_first
    sy_send[0, 1] = ex_last - p1[across(ny - 1), :] * 0.03125
    for k in range(1, m):
        y_copy(1, k, sy_send.at[0], sy_recv.at[0]).start()

    arrived(has_left, send_hz, hz_prev)

    def ey_one(i, hz_last):
        s = plane(i)
        hz_here = fields[HZ, s, :]
        ey1[s, :] = fields[EY, s, :] + ce[s, :] * (
            0.015625 * b_z(fields[HX, s, :]) - (hz_here - hz_last)
        )
        return hz_here

    lax.fori_loop(0, nx, ey_one, hz_prev[...])

    def reduce_matrix(me, count, wait, recv, own, one_ref, two_ref, coef, zero):
        def up(j, b):
            wait(j)
            rf = recv[j, 2]
            g = rf / (1.0 - b * recv[j, 0])
            one_ref[j] = g
            two_ref[j] = b
            return recv[j, 1] + g * b * rf

        b = lax.fori_loop(0, me, up, zero)

        def down(t, e):
            j = count - 1 - t
            wait(j)
            rf = recv[j, 2]
            h = rf / (1.0 - e * recv[j, 1])
            one_ref[j] = h
            two_ref[j] = e
            return recv[j, 0] + h * e * rf

        e = lax.fori_loop(0, count - 1 - me, down, zero)
        rf = own[2]
        one = 1.0 - b * own[0]
        two = 1.0 - e * own[1]
        scale = 1.0 / (one * two - (b * rf) * (e * rf))
        coef[0] = b
        coef[1] = e
        coef[2] = two * scale
        coef[3] = b * rf * scale
        coef[4] = e * rf * scale
        coef[5] = one * scale

    reduce_matrix(gx, n, lambda j: x_wait(0, mx_send, mx_recv, j),
                  mx_recv, mx_send, gx_one, gx_two, coef_x, zero_plane)
    reduce_matrix(gy, m, lambda j: y_wait(0, my_send, my_recv, j),
                  my_recv, my_send, gy_one, gy_two, coef_y, zero_row)

    def reduce_sides(me, count, wait, recv, own, one_ref, two_ref, coef, zero):
        def up(j, a):
            wait(j)
            return recv[j, 1] + one_ref[j] * (a + two_ref[j] * recv[j, 0])

        a = lax.fori_loop(0, me, up, zero)

        def down(t, c):
            j = count - 1 - t
            wait(j)
            return recv[j, 0] + one_ref[j] * (c + two_ref[j] * recv[j, 1])

        c = lax.fori_loop(0, count - 1 - me, down, zero)
        a = a + coef[0] * own[0]
        c = c + coef[1] * own[1]
        return coef[2] * a + coef[3] * c, coef[4] * a + coef[5] * c

    def x_sides(step):
        return reduce_sides(
            gx, n, lambda j: x_wait(1 + step, sx_send.at[step], sx_recv.at[step], j),
            sx_recv.at[step], sx_send.at[step], gx_one, gx_two, coef_x, zero_plane)

    def y_sides(step):
        return reduce_sides(
            gy, m, lambda j: y_wait(1 + step, sy_send.at[step], sy_recv.at[step], j),
            sy_recv.at[step], sy_send.at[step], gy_one, gy_two, coef_y, zero_row)

    wl, wr = x_sides(0)
    wr_x[...] = wr

    def ez_fill(i, _):
        s = plane(i)
        ez1[s, :] = p_x[s, :] + l_x[s, :] * wl + r_x[s, :] * wr
        return 0

    lax.fori_loop(0, nx, ez_fill, 0)
    ez_send[...] = ez1[across(0), :]
    start(has_low, send_ez)

    wl, wr = y_sides(0)
    wr_y[...] = wr

    def ex_fill(j, _):
        s = row(j)
        ex1[across(j), :] = p_y[s, :] + l_y[s, :] * wl + r_y[s, :] * wr
        return 0

    lax.fori_loop(0, ny, ex_fill, 0)

    def v_right(i, _):
        s = plane(i)
        g = f_z(ey1[s, :])
        rhs[s, :] = (
            3.0 * ez1[s, :] - fields[EZ, s, :] - ce[s, :] * b_y(g, 0.0)
        )
        out[HX, s, :] = fields[HX, s, :] + g
        return 0

    lax.fori_loop(0, nx, v_right, 0)
    v_first, v_last = y_sweep()
    sy_send[1, 0] = v_first
    sy_send[1, 1] = v_last + 0.03125 * (
        out[HX, across(ny - 1), :] - fields[HX, across(ny - 1), :]
    )
    for k in range(1, m):
        y_copy(2, k, sy_send.at[1], sy_recv.at[1]).start()

    arrived(has_high, send_ez, ez_next)

    def ey_forward(i, carry):
        p_last, d_last = carry
        s = plane(i)
        one = pl.ds(i, 1)
        p = p1[s, :] + 64.0 * f_y(ex1[s, :], wr_y[one, :])
        p2[s, :] = p
        ey = ey1[s, :]
        hx = fields[HX, s, :] - 32.0 * f_y(ez1[s, :], ez_next[one, :]) + 0.5 * f_z(ey)
        r = ey + ce[s, :] * (0.015625 * b_z(hx) - (p - p_last))
        d = r * inv_x[s, :] + c_x[s, :] * d_last
        p_x[s, :] = d
        return p, d

    p_end, ey_last = lax.fori_loop(0, nx, ey_forward, (zero_plane, zero_plane))
    sx_send[1, 0] = backward_sweep(nx, plane, zero_plane, c_x, p_x)
    sx_send[1, 1] = ey_last + p_end * 0.03125
    for k in range(1, n):
        x_copy(2, k, sx_send.at[1], sx_recv.at[1]).start()

    def ex_two(i, ez_after):
        i = nx - 1 - i
        s = plane(i)
        ex = fields[EX, s, :]
        ez_here = ez1[s, :]
        d_ex = 0.5 * f_z(ex)
        change = d_ex - 32.0 * (ez_after - ez_here)
        two = 2.0 * ex1[s, :] - ex + (0.015625 * ce[s, :]) * b_z(change)
        out[EX, s, :] = two
        out[HY, s, :] = fields[HY, s, :] - d_ex - 0.5 * f_z(two)
        return ez_here

    lax.fori_loop(0, nx, ex_two, wr_x[...])

    wl, wr = y_sides(1)
    wr_y[...] = wr

    def v_fill(j, _):
        s = row(j)
        rhs[across(j), :] = p_y[s, :] + l_y[s, :] * wl + r_y[s, :] * wr
        return 0

    lax.fori_loop(0, ny, v_fill, 0)
    start(has_left, send_v)

    def last_ez(i, _):
        s = plane(i)
        v = rhs[s, :]
        out[EZ, s, :] = v - ez1[s, :]
        out[HX, s, :] = out[HX, s, :] - 32.0 * f_y(v, wr_y[pl.ds(i, 1), :])
        return 0

    lax.fori_loop(0, nx, last_ez, 0)

    wl, wr = x_sides(1)

    def last_ey(t, after):
        s = plane(nx - 1 - t)
        w = p_x[s, :] + l_x[s, :] * wl + r_x[s, :] * wr
        out[EY, s, :] = w
        out[HZ, s, :] = p2[s, :] - 32.0 * (after - w)
        return w

    lax.fori_loop(0, nx, last_ey, wr)

    arrived(has_right, send_v, v_next)

    def last_hy(t, after):
        s = plane(nx - 1 - t)
        v = rhs[s, :]
        out[HY, s, :] = out[HY, s, :] + 32.0 * (after - v)
        return v

    lax.fori_loop(0, nx, last_hy, v_next[...])

    sent(has_left, send_ey)
    sent(has_right, send_hz)
    sent(has_high, send_hx)
    sent(has_low, send_ez)
    sent(has_left, send_v)
    for k in range(1, n):
        x_copy(0, k, mx_send, mx_recv).wait_send()
        x_copy(1, k, sx_send.at[0], sx_recv.at[0]).wait_send()
        x_copy(2, k, sx_send.at[1], sx_recv.at[1]).wait_send()
    for k in range(1, m):
        y_copy(0, k, my_send, my_recv).wait_send()
        y_copy(1, k, sy_send.at[0], sy_recv.at[0]).wait_send()
        y_copy(2, k, sy_send.at[1], sy_recv.at[1]).wait_send()


def local(n, m, fields, region, eps_table):
    _, nx, ny, nz = fields.shape
    cells = nx * ny
    labels = eps_table.shape[0]
    big = pltpu.VMEM((cells, nz), jnp.float32)
    x_row = pltpu.VMEM((ny, nz), jnp.float32)
    y_row = pltpu.VMEM((nx, nz), jnp.float32)

    def sided(width, count):
        return [
            pltpu.VMEM((3, width, nz), jnp.float32),
            pltpu.VMEM((count, 3, width, nz), jnp.float32),
            pltpu.VMEM((count, width, nz), jnp.float32),
            pltpu.VMEM((count, width, nz), jnp.float32),
            pltpu.VMEM((6, width, nz), jnp.float32),
            pltpu.VMEM((2, 2, width, nz), jnp.float32),
            pltpu.VMEM((2, count, 2, width, nz), jnp.float32),
        ]

    vmem = pl.BlockSpec(memory_space=pltpu.VMEM)
    result = pl.pallas_call(
        functools.partial(kernel, n, m, nx, ny, nz, labels),
        out_shape=jax.ShapeDtypeStruct((6, cells, nz), jnp.float32),
        in_specs=[vmem, vmem, pl.BlockSpec(memory_space=pltpu.SMEM)],
        out_specs=vmem,
        scratch_shapes=[big] * 17
        + [x_row, x_row, y_row, y_row, y_row, y_row, x_row, x_row, y_row]
        + sided(ny, n)
        + sided(nx, m)
        + [
            pltpu.SemaphoreType.DMA((5,)),
            pltpu.SemaphoreType.DMA((5,)),
            pltpu.SemaphoreType.DMA((3, n)),
            pltpu.SemaphoreType.DMA((3, n)),
            pltpu.SemaphoreType.DMA((3, m)),
            pltpu.SemaphoreType.DMA((3, m)),
        ],
        compiler_params=pltpu.CompilerParams(
            collective_id=0, has_side_effects=True, vmem_limit_bytes=40 * 1024 * 1024
        ),
    )(fields.reshape(6, cells, nz), region.reshape(cells, nz), eps_table)
    return result.reshape(fields.shape)


def solution(mesh):
    return jax.shard_map(
        functools.partial(local, mesh.shape["gx"], mesh.shape["gy"]),
        mesh=mesh,
        in_specs=(P(None, "gx", "gy", None), P("gx", "gy", None), P()),
        out_specs=P(None, "gx", "gy", None),
        check_vma=False,
    )
```

time: 259 us -> 32 us (0.12)
  the two profiles are of different devices: /device:TPU:3 before, /device:TPU:1 now
where the time goes in v1:
time: 32 us; the launch traced here: 31.8 us
  Pallas kernels  27.7 us (87%)
  local copies, waits for them, and re-layouts  4.16 us (13%)
    pallas_call x1, Pallas kernels, local(): pl.pallas_call(functools.partial(kernel, n, m, nx, ny, nz, labels), out_s...  27.7 us
    unnamed x7, local copies, waits for them, and re-layouts  4.16 us

profile of v1, /device:TPU:1, one launch (start us, length us, event | category | flops | bytes accessed | tf_op | source)
XLA Modules:
  0.0 31.8 jit_solution(17976144073701077334)
XLA Ops:
  0.0 0.0 copy-start
  0.0 1.4 %copy-done = f32[6,16,32,128]{3,2,1,0:T(8,128)S(1)} copy-done((f32[6,16,32,128]{3,2,1,0:T(8,128)S(1)}, f32[6,16,32,128]{3,2,1,0:T(8,128)}, u32[]{:S(2)}) %copy-start) | copy-done | bytes 1572888
  1.4 0.0 copy-start.1
  1.4 0.9 %copy-done.1 = s32[16,32,128]{2,1,0:T(8,128)S(1)} copy-done((s32[16,32,128]{2,1,0:T(8,128)S(1)}, s32[16,32,128]{2,1,0:T(8,128)}, u32[]{:S(2)}) %copy-start.1) | copy-done | bytes 262168
  2.4 0.0 copy-start.2
  2.4 0.7 %copy-done.2 = f32[16]{0:T(128)S(1)} copy-done((f32[16]{0:T(128)S(1)}, f32[16]{0:T(128)}, u32[]{:S(2)}) %copy-start.2) | copy-done | bytes 88
  3.0 27.7 %shard_map.37 = f32[6,512,128]{2,1,0:T(8,128)S(1)} custom-call(f32[6,512,128]{2,1,0:T(8,128)S(1)} %bitcast.4, s32[512,128]{1,0:T(8,128)S(1)} %bitcast.5, f32[16]{0:T(128)S(1)} %copy-done.2), custom_call_target="tpu_custom_call" | custom-call | tf_op jit(solution)/shard_map/pallas_call | solution.py:482
  30.7 1.1 %copy.5 = f32[6,16,32,128]{3,2,1,0:T(8,128)} copy(f32[6,16,32,128]{3,2,1,0:T(8,128)S(1)} %bitcast.3) | data formatting | bytes 3145728
Async XLA Ops:
  0.0 1.4 %copy-start = (f32[6,16,32,128]{3,2,1,0:T(8,128)S(1)}, f32[6,16,32,128]{3,2,1,0:T(8,128)}, u32[]{:S(2)}) copy-start(f32[6,16,32,128]{3,2,1,0:T(8,128)} %param.3) | copy-start | bytes 4718596
  1.4 0.9 %copy-start.1 = (s32[16,32,128]{2,1,0:T(8,128)S(1)}, s32[16,32,128]{2,1,0:T(8,128)}, u32[]{:S(2)}) copy-start(s32[16,32,128]{2,1,0:T(8,128)} %param.4) | copy-start | bytes 786436
  2.4 0.7 %copy-start.2 = (f32[16]{0:T(128)S(1)}, f32[16]{0:T(128)}, u32[]{:S(2)}) copy-start(f32[16]{0:T(128)} %eps.1) | copy-start | bytes 196

commit v2 on v1

--- a/solution.py
+++ b/solution.py
@@ -14,7 +14,7 @@
 def kernel(
     n, m, nx, ny, nz, labels,
     fields, region, eps, out,
-    ce, inv_x, c_x, l_x, r_x, inv_y, c_y, l_y, r_y,
+    ce, small_k, inv_x, c_x, l_x, r_x, inv_y, c_y, l_y, r_y,
     p_x, p_y, rhs, p1, ey1, ez1, ex1, p2,
     ey_next, hz_prev, hx_prev, hx_send, ez_next, ez_send, v_next, wr_x, wr_y,
     mx_send, mx_recv, gx_one, gx_two, coef_x, sx_send, sx_recv,
@@ -42,6 +42,9 @@
 
     def across(j):
         return pl.ds(j, nx, stride=ny)
+
+    def loop(count, body, init):
+        return lax.fori_loop(0, count, body, init, unroll=4)
 
     lane = lax.broadcasted_iota(jnp.int32, (ny, nz), 1)
     sub = lax.broadcasted_iota(jnp.int32, (ny, nz), 0)
@@ -146,27 +149,29 @@
     def coefficients(i, _):
         s = plane(i)
         label = region[s, :]
-        ce[s, :] = 32.0 / pick(label, 0, labels)
+        eps_here = pick(label, 0, labels)
+        small_k[s, :] = eps_here * (1.0 / 1024.0)
+        ce[s, :] = 32.0 / eps_here
         return 0
 
-    lax.fori_loop(0, nx, coefficients, 0)
-
-    def factor(count, load_ce, at, first, zero, inv_ref, c_ref, l_ref, r_ref, send_ref):
+    loop(nx, coefficients, 0)
+
+    def factor(count, load_small, at, first, zero, inv_ref, c_ref, l_ref, r_ref, send_ref):
         ones = zero + 1.0
 
         def forward(i, carry):
-            c_last, d_last = carry
-            kk = 32.0 * load_ce(i)
-            inv = 1.0 / (1.0 + (2.0 * kk - kk * c_last))
-            c = kk * inv
+            gap, d_last = carry
+            small = load_small(i)
+            total = small + gap
+            c = 1.0 / (1.0 + total)
             d = c * d_last
             s = at(i)
-            inv_ref[s, :] = inv
+            inv_ref[s, :] = c * small
             c_ref[s, :] = c
             l_ref[s, :] = d
-            return c, d
-
-        lax.fori_loop(0, count, forward, (zero + jnp.where(first, 1.0, 0.0), ones))
+            return total * c, d
+
+        loop(count, forward, (zero + jnp.where(first, 0.0, 1.0), ones))
 
         def backward(t, carry):
             l_after, r_after = carry
@@ -178,16 +183,16 @@
             r_ref[s, :] = r
             return l, r
 
-        l_first, r_first = lax.fori_loop(0, count, backward, (zero, ones))
+        l_first, r_first = loop(count, backward, (zero, ones))
         send_ref[0] = l_first
         send_ref[1] = r_ref[at(count - 1), :]
         send_ref[2] = r_first
 
-    factor(nx, lambda i: ce[plane(i), :], plane, gx == 0, zero_plane,
+    factor(nx, lambda i: small_k[plane(i), :], plane, gx == 0, zero_plane,
            inv_x, c_x, l_x, r_x, mx_send)
     for k in range(1, n):
         x_copy(0, k, mx_send, mx_recv).start()
-    factor(ny, lambda j: ce[across(j), :], row, gy == 0, zero_row,
+    factor(ny, lambda j: small_k[across(j), :], row, gy == 0, zero_row,
            inv_y, c_y, l_y, r_y, my_send)
     for k in range(1, m):
         y_copy(0, k, my_send, my_recv).start()
@@ -199,7 +204,7 @@
             p_ref[s, :] = w
             return w
 
-        return lax.fori_loop(0, count, body, zero)
+        return loop(count, body, zero)
 
     def y_sweep():
         def body(j, last):
@@ -208,7 +213,7 @@
             p_y[s, :] = d
             return d
 
-        last = lax.fori_loop(0, ny, body, zero_row)
+        last = loop(ny, body, zero_row)
         return backward_sweep(ny, row, zero_row, c_y, p_y), last
 
     arrived(has_low, send_hx, hx_prev)
@@ -225,7 +230,7 @@
         p_x[s, :] = d
         return q, d
 
-    q_end, ez_last = lax.fori_loop(0, nx, ez_forward, (zero_plane, zero_plane))
+    q_end, ez_last = loop(nx, ez_forward, (zero_plane, zero_plane))
     sx_send[0, 0] = backward_sweep(nx, plane, zero_plane, c_x, p_x)
     sx_send[0, 1] = ez_last - q_end * 0.03125
     for k in range(1, n):
@@ -245,7 +250,7 @@
         )
         return ey_here
 
-    lax.fori_loop(0, nx, ex_right, ey_next[...])
+    loop(nx, ex_right, ey_next[...])
     ex_first, ex_last = y_sweep()
     sy_send[0, 0] = ex_first
     sy_send[0, 1] = ex_last - p1[across(ny - 1), :] * 0.03125
@@ -262,7 +267,7 @@
         )
         return hz_here
 
-    lax.fori_loop(0, nx, ey_one, hz_prev[...])
+    loop(nx, ey_one, hz_prev[...])
 
     def reduce_matrix(me, count, wait, recv, own, one_ref, two_ref, coef, zero):
         def up(j, b):
@@ -336,7 +341,7 @@
         ez1[s, :] = p_x[s, :] + l_x[s, :] * wl + r_x[s, :] * wr
         return 0
 
-    lax.fori_loop(0, nx, ez_fill, 0)
+    loop(nx, ez_fill, 0)
     ez_send[...] = ez1[across(0), :]
     start(has_low, send_ez)
 
@@ -348,7 +353,7 @@
         ex1[across(j), :] = p_y[s, :] + l_y[s, :] * wl + r_y[s, :] * wr
         return 0
 
-    lax.fori_loop(0, ny, ex_fill, 0)
+    loop(ny, ex_fill, 0)
 
     def v_right(i, _):
         s = plane(i)
@@ -359,7 +364,7 @@
         out[HX, s, :] = fields[HX, s, :] + g
         return 0
 
-    lax.fori_loop(0, nx, v_right, 0)
+    loop(nx, v_right, 0)
     v_first, v_last = y_sweep()
     sy_send[1, 0] = v_first
     sy_send[1, 1] = v_last + 0.03125 * (
@@ -383,7 +388,7 @@
         p_x[s, :] = d
         return p, d
 
-    p_end, ey_last = lax.fori_loop(0, nx, ey_forward, (zero_plane, zero_plane))
+    p_end, ey_last = loop(nx, ey_forward, (zero_plane, zero_plane))
     sx_send[1, 0] = backward_sweep(nx, plane, zero_plane, c_x, p_x)
     sx_send[1, 1] = ey_last + p_end * 0.03125
     for k in range(1, n):
@@ -401,7 +406,7 @@
         out[HY, s, :] = fields[HY, s, :] - d_ex - 0.5 * f_z(two)
         return ez_here
 
-    lax.fori_loop(0, nx, ex_two, wr_x[...])
+    loop(nx, ex_two, wr_x[...])
 
     wl, wr = y_sides(1)
     wr_y[...] = wr
@@ -411,7 +416,7 @@
         rhs[across(j), :] = p_y[s, :] + l_y[s, :] * wl + r_y[s, :] * wr
         return 0
 
-    lax.fori_loop(0, ny, v_fill, 0)
+    loop(ny, v_fill, 0)
     start(has_left, send_v)
 
     def last_ez(i, _):
@@ -421,7 +426,7 @@
         out[HX, s, :] = out[HX, s, :] - 32.0 * f_y(v, wr_y[pl.ds(i, 1), :])
         return 0
 
-    lax.fori_loop(0, nx, last_ez, 0)
+    loop(nx, last_ez, 0)
 
     wl, wr = x_sides(1)
 
@@ -432,7 +437,7 @@
         out[HZ, s, :] = p2[s, :] - 32.0 * (after - w)
         return w
 
-    lax.fori_loop(0, nx, last_ey, wr)
+    loop(nx, last_ey, wr)
 
     arrived(has_right, send_v, v_next)
 
@@ -442,7 +447,7 @@
         out[HY, s, :] = out[HY, s, :] + 32.0 * (after - v)
         return v
 
-    lax.fori_loop(0, nx, last_hy, v_next[...])
+    loop(nx, last_hy, v_next[...])
 
     sent(has_left, send_ey)
     sent(has_right, send_hz)
@@ -484,7 +489,7 @@
         out_shape=jax.ShapeDtypeStruct((6, cells, nz), jnp.float32),
         in_specs=[vmem, vmem, pl.BlockSpec(memory_space=pltpu.SMEM)],
         out_specs=vmem,
-        scratch_shapes=[big] * 17
+        scratch_shapes=[big] * 18
         + [x_row, x_row, y_row, y_row, y_row, y_row, x_row, x_row, y_row]
         + sided(ny, n)
         + sided(nx, m)

time: 32 us -> 27.9 us (0.87)
  Pallas kernels: 27.7 us -> 23.5 us
    pallas_call x1, Pallas kernels: 27.7 us -> 23.5 us  [local(): pl.pallas_call(functools.partial(kernel, n, m, nx, ny, nz, labels), out_s...]
where the time goes in v2:
time: 27.9 us; the launch traced here: 27.7 us
  Pallas kernels  23.5 us (84%)
  local copies, waits for them, and re-layouts  4.16 us (15%)
    pallas_call x1, Pallas kernels, local(): pl.pallas_call(functools.partial(kernel, n, m, nx, ny, nz, labels), out_s...  23.5 us
    unnamed x7, local copies, waits for them, and re-layouts  4.16 us

profile of v2, /device:TPU:1, one launch (start us, length us, event | category | flops | bytes accessed | tf_op | source)
XLA Modules:
  0.0 27.7 jit_solution(6282381945803914932)
XLA Ops:
  0.0 0.0 copy-start
  0.0 1.4 %copy-done = f32[6,16,32,128]{3,2,1,0:T(8,128)S(1)} copy-done((f32[6,16,32,128]{3,2,1,0:T(8,128)S(1)}, f32[6,16,32,128]{3,2,1,0:T(8,128)}, u32[]{:S(2)}) %copy-start) | copy-done | bytes 1572888
  1.4 0.0 copy-start.1
  1.4 0.9 %copy-done.1 = s32[16,32,128]{2,1,0:T(8,128)S(1)} copy-done((s32[16,32,128]{2,1,0:T(8,128)S(1)}, s32[16,32,128]{2,1,0:T(8,128)}, u32[]{:S(2)}) %copy-start.1) | copy-done | bytes 262168
  2.4 0.0 copy-start.2
  2.4 0.7 %copy-done.2 = f32[16]{0:T(128)S(1)} copy-done((f32[16]{0:T(128)S(1)}, f32[16]{0:T(128)}, u32[]{:S(2)}) %copy-start.2) | copy-done | bytes 88
  3.0 23.5 %shard_map.37 = f32[6,512,128]{2,1,0:T(8,128)S(1)} custom-call(f32[6,512,128]{2,1,0:T(8,128)S(1)} %bitcast.4, s32[512,128]{1,0:T(8,128)S(1)} %bitcast.5, f32[16]{0:T(128)S(1)} %copy-done.2), custom_call_target="tpu_custom_call" | custom-call | tf_op jit(solution)/shard_map/pallas_call | solution.py:487
  26.6 1.1 %copy.5 = f32[6,16,32,128]{3,2,1,0:T(8,128)} copy(f32[6,16,32,128]{3,2,1,0:T(8,128)S(1)} %bitcast.3) | data formatting | bytes 3145728
Async XLA Ops:
  0.0 1.4 %copy-start = (f32[6,16,32,128]{3,2,1,0:T(8,128)S(1)}, f32[6,16,32,128]{3,2,1,0:T(8,128)}, u32[]{:S(2)}) copy-start(f32[6,16,32,128]{3,2,1,0:T(8,128)} %param.3) | copy-start | bytes 4718596
  1.4 0.9 %copy-start.1 = (s32[16,32,128]{2,1,0:T(8,128)S(1)}, s32[16,32,128]{2,1,0:T(8,128)}, u32[]{:S(2)}) copy-start(s32[16,32,128]{2,1,0:T(8,128)} %param.4) | copy-start | bytes 786436
  2.4 0.7 %copy-start.2 = (f32[16]{0:T(128)S(1)}, f32[16]{0:T(128)}, u32[]{:S(2)}) copy-start(f32[16]{0:T(128)} %eps.1) | copy-start | bytes 196

commit v3 on v2

--- a/solution.py
+++ b/solution.py
@@ -13,18 +13,27 @@
 
 def kernel(
     n, m, nx, ny, nz, labels,
-    fields, region, eps, out,
+    fields_in, region_in, eps_in, out, fields, region, eps,
     ce, small_k, inv_x, c_x, l_x, r_x, inv_y, c_y, l_y, r_y,
     p_x, p_y, rhs, p1, ey1, ez1, ex1, p2,
     ey_next, hz_prev, hx_prev, hx_send, ez_next, ez_send, v_next, wr_x, wr_y,
     mx_send, mx_recv, gx_one, gx_two, coef_x, sx_send, sx_recv,
     my_send, my_recv, gy_one, gy_two, coef_y, sy_send, sy_recv,
-    near_send, near_recv, x_send, x_recv, y_send, y_recv,
+    load_sem, near_send, near_recv, x_send, x_recv, y_send, y_recv,
 ):
     gx = lax.axis_index("gx")
     gy = lax.axis_index("gy")
 
+    load_eps = pltpu.make_async_copy(eps_in, eps, load_sem.at[7])
+    load_region = pltpu.make_async_copy(region_in, region, load_sem.at[6])
+    loads = [
+        pltpu.make_async_copy(fields_in.at[f], fields.at[f], load_sem.at[f]) for f in range(6)
+    ]
     barrier = pltpu.get_barrier_semaphore()
+    load_eps.start()
+    load_region.start()
+    for f in (HX, EY, HZ, EX, HY, EZ):
+        loads[f].start()
     for k in range(1, n):
         pl.semaphore_signal(
             barrier, inc=1, device_id={"gx": lax.rem(gx + k, n)}, device_id_type=MESH
@@ -103,7 +112,6 @@
         def _():
             ref[...] = jnp.zeros(ref.shape, jnp.float32)
 
-    hx_send[...] = fields[HX, across(ny - 1), :]
 
     def x_copy(kind, k, src, dst):
         target = lax.rem(gx + k, n)
@@ -130,11 +138,6 @@
             src_ref=src, dst_ref=dst.at[j], send_sem=y_send.at[kind, 0],
             recv_sem=y_recv.at[kind, j], device_id={"gy": j}, device_id_type=MESH,
         ).wait_recv()
-
-    pl.semaphore_wait(barrier, n + m - 2)
-    start(has_left, send_ey)
-    start(has_high, send_hx)
-    start(has_right, send_hz)
 
     def pick(label, lowest, width):
         if width == 1:
@@ -154,46 +157,70 @@
         ce[s, :] = 32.0 / eps_here
         return 0
 
+    load_eps.wait()
+    load_region.wait()
     loop(nx, coefficients, 0)
-
-    def factor(count, load_small, at, first, zero, inv_ref, c_ref, l_ref, r_ref, send_ref):
-        ones = zero + 1.0
-
-        def forward(i, carry):
-            gap, d_last = carry
-            small = load_small(i)
-            total = small + gap
-            c = 1.0 / (1.0 + total)
-            d = c * d_last
-            s = at(i)
-            inv_ref[s, :] = c * small
-            c_ref[s, :] = c
-            l_ref[s, :] = d
-            return total * c, d
-
-        loop(count, forward, (zero + jnp.where(first, 0.0, 1.0), ones))
-
-        def backward(t, carry):
-            l_after, r_after = carry
-            s = at(count - 1 - t)
-            c = c_ref[s, :]
-            l = l_ref[s, :] + c * l_after
-            r = c * r_after
-            l_ref[s, :] = l
-            r_ref[s, :] = r
-            return l, r
-
-        l_first, r_first = loop(count, backward, (zero, ones))
-        send_ref[0] = l_first
-        send_ref[1] = r_ref[at(count - 1), :]
-        send_ref[2] = r_first
-
-    factor(nx, lambda i: small_k[plane(i), :], plane, gx == 0, zero_plane,
-           inv_x, c_x, l_x, r_x, mx_send)
+    pl.semaphore_wait(barrier, n + m - 2)
+    loads[HX].wait()
+    hx_send[...] = fields[HX, across(ny - 1), :]
+    start(has_high, send_hx)
+    loads[EY].wait()
+    start(has_left, send_ey)
+    loads[HZ].wait()
+    start(has_right, send_hz)
+
+    per = ny // nx
+
+    def factor_step(small, carry, s, inv_ref, c_ref, l_ref):
+        gap, d_last = carry
+        total = small + gap
+        c = 1.0 / (1.0 + total)
+        d = c * d_last
+        inv_ref[s, :] = c * small
+        c_ref[s, :] = c
+        l_ref[s, :] = d
+        return total * c, d
+
+    def factor_forward(i, carry):
+        on_x, on_y = carry
+        on_x = factor_step(small_k[plane(i), :], on_x, plane(i), inv_x, c_x, l_x)
+        for k in range(per):
+            j = i * per + k
+            on_y = factor_step(small_k[across(j), :], on_y, row(j), inv_y, c_y, l_y)
+        return on_x, on_y
+
+    loop(nx, factor_forward, (
+        (zero_plane + jnp.where(gx == 0, 0.0, 1.0), zero_plane + 1.0),
+        (zero_row + jnp.where(gy == 0, 0.0, 1.0), zero_row + 1.0),
+    ))
+
+    def factor_back(carry, s, c_ref, l_ref, r_ref):
+        l_after, r_after = carry
+        c = c_ref[s, :]
+        l = l_ref[s, :] + c * l_after
+        r = c * r_after
+        l_ref[s, :] = l
+        r_ref[s, :] = r
+        return l, r
+
+    def factor_backward(t, carry):
+        on_x, on_y = carry
+        on_x = factor_back(on_x, plane(nx - 1 - t), c_x, l_x, r_x)
+        for k in range(per):
+            on_y = factor_back(on_y, row(ny - 1 - t * per - k), c_y, l_y, r_y)
+        return on_x, on_y
+
+    on_x, on_y = loop(
+        nx, factor_backward, ((zero_plane, zero_plane + 1.0), (zero_row, zero_row + 1.0))
+    )
+    mx_send[0] = on_x[0]
+    mx_send[1] = r_x[plane(nx - 1), :]
+    mx_send[2] = on_x[1]
     for k in range(1, n):
         x_copy(0, k, mx_send, mx_recv).start()
-    factor(ny, lambda j: small_k[across(j), :], row, gy == 0, zero_row,
-           inv_y, c_y, l_y, r_y, my_send)
+    my_send[0] = on_y[0]
+    my_send[1] = r_y[row(ny - 1), :]
+    my_send[2] = on_y[1]
     for k in range(1, m):
         y_copy(0, k, my_send, my_recv).start()
 
@@ -216,6 +243,9 @@
         last = loop(ny, body, zero_row)
         return backward_sweep(ny, row, zero_row, c_y, p_y), last
 
+    loads[EX].wait()
+    loads[HY].wait()
+    loads[EZ].wait()
     arrived(has_low, send_hx, hx_prev)
 
     def ez_forward(i, carry):
@@ -486,14 +516,20 @@
     vmem = pl.BlockSpec(memory_space=pltpu.VMEM)
     result = pl.pallas_call(
         functools.partial(kernel, n, m, nx, ny, nz, labels),
-        out_shape=jax.ShapeDtypeStruct((6, cells, nz), jnp.float32),
-        in_specs=[vmem, vmem, pl.BlockSpec(memory_space=pltpu.SMEM)],
+        out_shape=pltpu.VMEM((6, cells, nz), jnp.float32),
+        in_specs=[pl.BlockSpec(memory_space=pl.ANY)] * 3,
         out_specs=vmem,
-        scratch_shapes=[big] * 18
+        scratch_shapes=[
+            pltpu.VMEM((6, cells, nz), jnp.float32),
+            pltpu.VMEM((cells, nz), jnp.int32),
+            pltpu.SMEM((labels,), jnp.float32),
+        ]
+        + [big] * 18
         + [x_row, x_row, y_row, y_row, y_row, y_row, x_row, x_row, y_row]
         + sided(ny, n)
         + sided(nx, m)
         + [
+            pltpu.SemaphoreType.DMA((8,)),
             pltpu.SemaphoreType.DMA((5,)),
             pltpu.SemaphoreType.DMA((5,)),
             pltpu.SemaphoreType.DMA((3, n)),
@@ -502,7 +538,7 @@
             pltpu.SemaphoreType.DMA((3, m)),
         ],
         compiler_params=pltpu.CompilerParams(
-            collective_id=0, has_side_effects=True, vmem_limit_bytes=40 * 1024 * 1024
+            collective_id=0, has_side_effects=True, vmem_limit_bytes=60 * 1024 * 1024
         ),
     )(fields.reshape(6, cells, nz), region.reshape(cells, nz), eps_table)
     return result.reshape(fields.shape)

time: 27.9 us -> 24.4 us (0.87)
  local copies, waits for them, and re-layouts: 4.16 us -> 1.15 us
  Pallas kernels: 23.5 us -> 23.1 us
    unnamed x7 -> x1, local copies, waits for them, and re-layouts: 4.16 us -> 1.15 us
    pallas_call x1, Pallas kernels: 23.5 us -> 23.1 us  [local(): pl.pallas_call(functools.partial(kernel, n, m, nx, ny, nz, labels), out_s...]
where the time goes in v3:
time: 24.4 us; the launch traced here: 24.3 us
  Pallas kernels  23.1 us (95%)
  local copies, waits for them, and re-layouts  1.15 us (5%)
    pallas_call x1, Pallas kernels, local(): pl.pallas_call(functools.partial(kernel, n, m, nx, ny, nz, labels), out_s...  23.1 us
    unnamed x1, local copies, waits for them, and re-layouts  1.15 us

profile of v3, /device:TPU:1, one launch (start us, length us, event | category | flops | bytes accessed | tf_op | source)
XLA Modules:
  0.0 24.3 jit_solution(8751267647878265342)
XLA Ops:
  0.0 23.1 %shard_map.37 = f32[6,512,128]{2,1,0:T(8,128)S(1)} custom-call(f32[6,512,128]{2,1,0:T(8,128)} %bitcast.4, s32[512,128]{1,0:T(8,128)} %bitcast.5, f32[16]{0:T(128)} %eps_in.1), custom_call_target="tpu_custom_call" | custom-call | tf_op jit(solution)/shard_map/pallas_call | solution.py:517
  23.1 1.1 %copy.5 = f32[6,16,32,128]{3,2,1,0:T(8,128)} copy(f32[6,16,32,128]{3,2,1,0:T(8,128)S(1)} %bitcast.3) | data formatting | bytes 3145728

commit v4 on v3

--- a/solution.py
+++ b/solution.py
@@ -53,7 +53,7 @@
         return pl.ds(j, nx, stride=ny)
 
     def loop(count, body, init):
-        return lax.fori_loop(0, count, body, init, unroll=4)
+        return lax.fori_loop(0, count, body, init, unroll=8)
 
     lane = lax.broadcasted_iota(jnp.int32, (ny, nz), 1)
     sub = lax.broadcasted_iota(jnp.int32, (ny, nz), 0)
@@ -395,14 +395,6 @@
         return 0
 
     loop(nx, v_right, 0)
-    v_first, v_last = y_sweep()
-    sy_send[1, 0] = v_first
-    sy_send[1, 1] = v_last + 0.03125 * (
-        out[HX, across(ny - 1), :] - fields[HX, across(ny - 1), :]
-    )
-    for k in range(1, m):
-        y_copy(2, k, sy_send.at[1], sy_recv.at[1]).start()
-
     arrived(has_high, send_ez, ez_next)
 
     def ey_forward(i, carry):
@@ -423,6 +415,14 @@
     sx_send[1, 1] = ey_last + p_end * 0.03125
     for k in range(1, n):
         x_copy(2, k, sx_send.at[1], sx_recv.at[1]).start()
+
+    v_first, v_last = y_sweep()
+    sy_send[1, 0] = v_first
+    sy_send[1, 1] = v_last + 0.03125 * (
+        out[HX, across(ny - 1), :] - fields[HX, across(ny - 1), :]
+    )
+    for k in range(1, m):
+        y_copy(2, k, sy_send.at[1], sy_recv.at[1]).start()
 
     def ex_two(i, ez_after):
         i = nx - 1 - i

time: 24.4 us -> 26.2 us (1.074)
  Pallas kernels: 23.1 us -> 24.9 us
    pallas_call x1, Pallas kernels: 23.1 us -> 24.9 us  [local(): pl.pallas_call(functools.partial(kernel, n, m, nx, ny, nz, labels), out_s...]
where the time goes in v4:
time: 26.2 us; the launch traced here: 26.1 us
  Pallas kernels  24.9 us (95%)
  local copies, waits for them, and re-layouts  1.15 us (4%)
    pallas_call x1, Pallas kernels, local(): pl.pallas_call(functools.partial(kernel, n, m, nx, ny, nz, labels), out_s...  24.9 us
    unnamed x1, local copies, waits for them, and re-layouts  1.15 us

profile of v4, /device:TPU:1, one launch (start us, length us, event | category | flops | bytes accessed | tf_op | source)
XLA Modules:
  0.0 26.1 jit_solution(13890094890343527859)
XLA Ops:
  0.0 24.9 %shard_map.37 = f32[6,512,128]{2,1,0:T(8,128)S(1)} custom-call(f32[6,512,128]{2,1,0:T(8,128)} %bitcast.4, s32[512,128]{1,0:T(8,128)} %bitcast.5, f32[16]{0:T(128)} %eps_in.1), custom_call_target="tpu_custom_call" | custom-call | tf_op jit(solution)/shard_map/pallas_call | solution.py:517
  25.0 1.1 %copy.5 = f32[6,16,32,128]{3,2,1,0:T(8,128)} copy(f32[6,16,32,128]{3,2,1,0:T(8,128)S(1)} %bitcast.3) | data formatting | bytes 3145728
